TPU v7x, 768 devices: a whole 4x8x12 slice. The times are simulated.
768 devices in a mesh: replica: 32 (over y, x), tok: 24 (over z, core).
Axes of the slice: x: 4, y: 8, z: 12, core: 2. Of those that a mesh axis runs over, the one named last changes fastest.
Arguments:
- activations: bfloat16 [196608, 2880], P(('replica', 'tok')), may hold values from -24 to 24
- cotangent: bfloat16 [196608, 512], P(('replica', 'tok')), may hold values from -6 to 6
- next_inputs: bfloat16 [196608, 2880], P(('replica', 'tok')), may hold values from -6 to 6
- weight_tiles: bfloat16 [360, 4096], P('tok'), may hold values from -0.109375 to 0.109375
- momentum: float32 [32, 360, 4096], P('replica', 'tok'), may hold values from -6 to 6
- chosen: int32 [32, 24, 8], P('replica', 'tok'), may hold values from 0 to 14, as said below
- counts: int32 [32, 24], P('replica', 'tok'), may hold values from 1 to 8, as said below
Outputs:
- values: bfloat16 [196608, 512], P(('replica', 'tok'))
- new_momentum: float32 [32, 360, 4096], P('replica', 'tok')
Inputs may be any that keep to these rules, and one draw needn't show every extreme that they name: Each list chosen[r, k] names 8 different tile numbers of the shard's 15 tiles; only the first counts[r, k] of them are selected. `counts`: in every draw some token shard has 8 selected tiles in every replica.
All inputs are finite; a program needn't handle non-finite values.
Results may differ from a plain program's by a relative error of at most 0.015.
Values may be sent and summed in bfloat16 or wider, within the bound.
A program may use at most 64 MiB of HBM per device.

v0:
```python
import math

import jax
import jax.numpy as jnp
from jax import lax
from jax.sharding import PartitionSpec as P

TILE = 64
KEEP = 32


momentum_decay = 0.9
step_size = 0.01


def cosine_rows(count):
    frequency = jnp.arange(count, dtype=jnp.float32)[:, None]
    position = jnp.arange(TILE, dtype=jnp.float32)[None, :]
    cosines = jnp.cos(math.pi * (2.0 * position + 1.0) * frequency / (2.0 * TILE))
    factor = jnp.where(frequency == 0, math.sqrt(1.0 / TILE), math.sqrt(2.0 / TILE))
    return cosines * factor


def rebuild(summed, weight_part, keep_rows):
    quads = summed.reshape(summed.shape[0], KEEP, KEEP)
    update = jnp.einsum(
        "ua,tuv,vb->tab", keep_rows, quads, keep_rows, precision=lax.Precision.HIGHEST
    )
    shifted = weight_part.astype(jnp.float32) - step_size * update.reshape(
        summed.shape[0], TILE * TILE
    )
    return shifted.astype(jnp.bfloat16)


def forward(inputs, new_tiles):
    row_tiles = inputs.shape[1] // TILE
    col_tiles = new_tiles.shape[0] // row_tiles
    blocks = inputs.reshape(inputs.shape[0], row_tiles, TILE)
    matrix = new_tiles.reshape(row_tiles, col_tiles, TILE, TILE)
    output = jnp.einsum("tra,rcab->tcb", blocks, matrix, preferred_element_type=jnp.float32)
    return output.reshape(inputs.shape[0], col_tiles * TILE).astype(jnp.bfloat16)


def local(activations, cotangent, next_inputs, weight_tiles, momentum, chosen, counts):
    highest = lax.Precision.HIGHEST
    shards = lax.axis_size("tok")
    tiles_here = weight_tiles.shape[0]
    row_tiles = activations.shape[1] // TILE
    col_tiles = cotangent.shape[1] // TILE
    grad_scale = 1.0 / math.sqrt(activations.shape[0] * shards)
    keep_rows = cosine_rows(KEEP)
    row_span = min(tiles_here * lax.axis_size("tok") // col_tiles + 2, row_tiles)
    product = (
        lax.dot_general(
            activations, cotangent, (((0,), (0,)), ((), ())), preferred_element_type=jnp.float32
        )
        * grad_scale
    )
    tiled = product.reshape(row_span, TILE, col_tiles, TILE).transpose(0, 2, 1, 3)
    tiled = tiled.reshape(row_span * col_tiles, TILE * TILE)
    gradient = lax.psum_scatter(
        tiled.astype(jnp.bfloat16), "tok", scatter_dimension=0, tiled=True
    ).astype(jnp.float32)
    updated = momentum_decay * momentum[0] + gradient
    chosen_here = chosen[0, 0]
    in_list = jnp.arange(chosen_here.shape[0], dtype=jnp.int32) < counts[0, 0]
    picked = jnp.take(updated, chosen_here, axis=0).reshape(-1, TILE, TILE)
    quadrant = jnp.einsum("ua,nab,vb->nuv", keep_rows, picked, keep_rows, precision=highest)
    quadrant = jnp.where(in_list[:, None, None], quadrant, 0.0).astype(jnp.bfloat16)
    rebuilt = jnp.einsum(
        "ua,nuv,vb->nab", keep_rows, quadrant.astype(jnp.float32), keep_rows, precision=highest
    )
    new_momentum = updated.at[chosen_here].add(-rebuilt.reshape(-1, TILE * TILE))
    listed = jnp.where(in_list, chosen_here, -1)
    flat_quads = quadrant.reshape(-1, KEEP * KEEP)
    tile_numbers = jnp.arange(tiles_here, dtype=jnp.int32)
    all_quads, all_listed = (
        lax.all_gather(flat_quads, "replica", axis=0, tiled=True),
        lax.all_gather(listed, "replica", axis=0, tiled=True),
    )
    one_hot = (all_listed[:, None] == tile_numbers[None, :]).astype(jnp.bfloat16)
    summed = lax.dot_general(
        one_hot, all_quads, (((0,), (0,)), ((), ())), preferred_element_type=jnp.float32
    )
    new_part = rebuild(summed, weight_tiles, keep_rows)
    new_full = lax.all_gather(new_part, "tok", axis=0, tiled=True)
    values = forward(next_inputs, new_full)
    return (values, new_momentum[None])


def solution(mesh):
    return jax.shard_map(
        local,
        mesh=mesh,
        in_specs=(
            P(("replica", "tok"), None),
            P(("replica", "tok"), None),
            P(("replica", "tok"), None),
            P("tok", None),
            P("replica", "tok", None),
            P("replica", "tok", None),
            P("replica", "tok"),
        ),
        out_specs=(P(("replica", "tok"), None), P("replica", "tok", None)),
        check_vma=False,
    )
```

profile of v0, /device:TPU:1, one launch (start us, length us, event | category | flops | bytes accessed | tf_op | source)
XLA Modules:
  0.0 254.2 jit_solution(6271214376289854712)
XLA Ops:
  7.2 1.3 copy-done
  8.5 3.5 %multiply_convert_fusion = bf16[2880,512]{1,0:T(8,128)(2,1)} fusion(bf16[256,2880]{0,1:T(8,128)(2,1)S(1)} %copy-done, bf16[256,512]{1,0:T(8,128)(2,1)} %param.8), kind=kOutput, calls=%fused_computation.2 | convolution fusion | flops 757923840 | bytes 4685824 | tf_op jit(solution)/shard_map/dot_general | solution.py:54
  12.1 8.4 %convert_element_type.37 = bf16[45,64,8,64]{3,2,1,0:T(8,128)(2,1)} reshape(bf16[2880,512]{1,0:T(8,128)(2,1)} %multiply_convert_fusion) | data formatting | bytes 5898240 | tf_op jit(solution)/shard_map/convert_element_type | solution.py:62
  20.5 7.0 %copy.19 = bf16[45,8,64,64]{3,2,1,0:T(8,128)(2,1)} copy(bf16[45,8,64,64]{3,1,2,0:T(8,128)(2,1)} %bitcast.60) | data formatting | bytes 5898240 | tf_op jit(solution)/shard_map/convert_element_type | solution.py:62
  27.5 8.7 %convert_element_type.39 = bf16[360,4096]{1,0:T(8,128)(2,1)} reshape(bf16[45,8,64,64]{3,2,1,0:T(8,128)(2,1)} %copy.19) | data formatting | bytes 5898240 | tf_op jit(solution)/shard_map/convert_element_type | solution.py:62
  36.2 54.8 %fusion = bf16[16,4096]{1,0:T(8,128)(2,1)S(1)} fusion(bf16[360,4096]{1,0:T(8,128)(2,1)} %convert_element_type.39), kind=kCustom, calls=%all-reduce-scatter | all-reduce-scatter fusion | flops 1572865 | bytes 3084288
  91.0 3.0 %collective-permute-start = (bf16[16,4096]{1,0:T(8,128)(2,1)S(1)}, bf16[16,4096]{1,0:T(8,128)(2,1)S(1)}, u32[]{:S(2)}, u32[]{:S(2)}) collective-permute-start(bf16[16,4096]{1,0:T(8,128)(2,1)S(1)} %fusion), channel_id=1, source_target_pairs={{0,1},{1,2},{2,3},{3,4},{4,5},{5,6},{6,7},{7,8},{8,9},{9,10},{10,1... | collective-permute-start | bytes 393224
  94.0 1.3 collective-permute-start.1
  96.1 1.3 dynamic-slice
  98.1 1.3 dynamic-slice.5
  100.0 16.6 %all-reduce = s32[256]{0:T(256)S(1)} all-reduce(s32[256]{0:T(256)S(1)} %fusion.37), channel_id=1, replica_groups=mesh['replica'=32,'tok'=24] {'replica'}, use_global_device_ids=true, to_apply=%add | all-reduce | flops 256 | bytes 2048
  116.7 0.6 concatenate
  117.5 0.6 gather_fusion
  119.1 35.6 %all_gather.10 = bf16[256,1024]{1,0:T(8,128)(2,1)S(1)} all-gather(bf16[8,1024]{1,0:T(8,128)(2,1)S(1)} %reshape.90), channel_id=1, replica_groups=mesh['replica'=32,'tok'=24] {'replica'}, dimensions={0}, use_global_device_ids=true | all-gather | bytes 540672 | tf_op jit(solution)/shard_map/all_gather | solution.py:78
  155.0 0.6 fusion.14
  155.6 1.0 convolution_multiply_fusion
  156.8 0.7 fusion.5
  157.8 0.6 convolution_negate_fusion
  158.6 1.1 scatter_fusion
  159.6 0.9 copy.24
  160.6 72.2 %all-gather.3.cloned.1.call-done = bf16[24,15,4096]{2,1,0:T(8,128)(2,1)} async-done(((bf16[1,15,4096]{2,1,0:T(8,128)(2,1)}), bf16[24,15,4096]{2,1,0:T(8,128)(2,1)}) %all-gather.3.cloned.1.call-update) | async-done | bytes 2949136 | tf_op jit(solution)/shard_map/all_gather | solution.py:86
  232.8 9.4 %reshape.92 = bf16[45,8,64,64]{3,2,1,0:T(8,128)(2,1)} reshape(bf16[24,15,4096]{2,1,0:T(8,128)(2,1)} %all-gather.3.cloned.1.call-done) | data formatting | bytes 5898240 | tf_op jit(solution)/shard_map/reshape | solution.py:39
  242.1 4.4 %fusion.1 = bf16[8,64,256]{2,1,0:T(8,128)(2,1)S(1)} fusion(bf16[45,8,64,64]{3,2,1,0:T(8,128)(2,1)} %reshape.92, bf16[256,45,64,1]{0,2,3,1:T(8,128)(2,1)S(1)} %bitcast.61), kind=kOutput, calls=%fused_computation.5 | convolution fusion | flops 755105792 | bytes 4685824 | tf_op jit(solution)/shard_map/tra,rcab->tcb/dot_general | solution.py:40
  246.5 0.8 copy.23
  (32 shorter events, 2.3 us)
Async XLA Ops:
  7.2 1.4 copy-start
  7.2 225.6 %all-gather.3.cloned.1.call-start = ((), (), s32[]{:S(2)}) async-start(), calls=%async_computation | async-start | bytes 3276800 | tf_op jit(solution)/shard_map/all_gather | solution.py:86
  36.2 59.2 %copy-start.4 = (s32[1,1,8]{2,1,0:T(1,128)S(1)}, s32[1,1,8]{2,1,0:T(1,128)}, u32[]{:S(2)}) copy-start(s32[1,1,8]{2,1,0:T(1,128)} %param.12) | copy-start | bytes 100
  36.2 81.1 %copy-start.2 = (f32[1,15,4096]{2,0,1:T(1,128)S(1)}, f32[1,15,4096]{2,0,1:T(1,128)}, u32[]{:S(2)}) copy-start(f32[1,15,4096]{2,0,1:T(1,128)} %param.11) | copy-start | bytes 737284
  91.0 25.7 %collective-permute-start = (bf16[16,4096]{1,0:T(8,128)(2,1)S(1)}, bf16[16,4096]{1,0:T(8,128)(2,1)S(1)}, u32[]{:S(2)}, u32[]{:S(2)}) collective-permute-start(bf16[16,4096]{1,0:T(8,128)(2,1)S(1)} %fusion), channel_id=1, source_target_pairs={{0,1},{1,2},{2,3},{3,4},{4,5},{5,6},{6,7},{7,8},{8,9},{9,10},{10,1... | collective-permute-start | bytes 393224
  94.0 22.7 %collective-permute-start.1 = (bf16[7,4096]{1,0:T(8,128)(2,1)S(1)}, bf16[7,4096]{1,0:T(8,128)(2,1)S(1)}, u32[]{:S(2)}, u32[]{:S(2)}) collective-permute-start(bf16[7,4096]{1,0:T(8,128)(2,1)S(1)} %slice.2), channel_id=1, source_target_pairs={{0,2},{1,3},{2,4},{3,5},{4,6},{5,7},{6,8},{7,9},{8,10},{9,11},{10,... | collective-permute-start | bytes 172040
  117.3 39.5 %copy-start.3 = (bf16[15,4096]{1,0:T(8,128)(2,1)S(1)}, bf16[15,4096]{1,0:T(8,128)(2,1)}, u32[]{:S(2)}) copy-start(bf16[15,4096]{1,0:T(8,128)(2,1)} %param.10) | copy-start | bytes 368644
  160.6 81.5 %copy-start.1 = (bf16[256,2880]{0,1:T(8,128)(2,1)S(1)}, bf16[256,2880]{0,1:T(8,128)(2,1)}, u32[]{:S(2)}) copy-start(bf16[256,2880]{0,1:T(8,128)(2,1)} %param.9) | copy-start | bytes 4423684
Sparse Core Ops, SparseCore 0:
  157.6 75.0 all-gather.2
where the time goes:
time: 255 us; the launch traced here: 254 us
  blocking collectives  107 us (42%)
  waiting for transfers between devices  72.2 us (28%)
  local copies, waits for them, and re-layouts  41 us (16%)
  between operations  16.2 us (6%)
  matrix products  11.4 us (4%)
  starting transfers between devices  4.33 us (2%)
    all_gather x1, waiting for transfers between devices, local(): new_full = lax.all_gather(new_part, 'tok', axis=0, tiled=True)  72.2 us
    unnamed x2, blocking collectives  71.4 us
    all_gather x1, blocking collectives, local(): lax.all_gather(flat_quads, 'replica', axis=0, tiled=True)  35.6 us
    convert_element_type x3, local copies, waits for them, and re-layouts, local(): tiled.astype(jnp.bfloat16)  24.1 us
    reshape x1, local copies, waits for them, and re-layouts, forward(): matrix = new_tiles.reshape(row_tiles, col_tiles, TILE, TILE)  9.35 us
    unnamed x17, local copies, waits for them, and re-layouts  6.31 us
  transfers between devices with their start and end apart: 3, of which 1 were waited for; matrix products, arithmetic and copies ran while one was open for 2% of the time, Pallas kernels for 0%

commit v1 on v0

v1 whole, which is shorter than its diff:
```python
import functools
import math

import jax
import jax.numpy as jnp
import numpy as np
from jax import lax
from jax.experimental import pallas as pl
from jax.experimental.pallas import tpu as pltpu
from jax.sharding import PartitionSpec as P

TILE = 64
KEEP = 32
CHIP_TILES = 30
CHIP_PAIRS = 15
PAIRS = 8
XS = 4

momentum_decay = 0.9
step_size = 0.01
F32 = jnp.float32
BF16 = jnp.bfloat16


def cosine_table():
    frequency = np.arange(KEEP)[:, None]
    position = np.arange(TILE)[None, :]
    cosines = np.cos(math.pi * (2.0 * position + 1.0) * frequency / (2.0 * TILE))
    factor = np.where(frequency == 0, math.sqrt(1.0 / TILE), math.sqrt(2.0 / TILE))
    return (cosines * factor).astype(np.float32)


def tables(col_tiles):
    low = cosine_table()
    fine = np.zeros((352, 128), np.float32)
    fine[0:32, 0:64] = low
    fine[32:96, 0:32] = low.T
    two = np.kron(np.eye(2, dtype=np.float32), low.T)
    fine[96:224, 0:64] = two
    fine[96:224, 64:128] = two
    fine[224:288, :] = two.T
    rows_low = np.kron(np.eye(4, dtype=np.float32), low.T)
    cols_low = np.kron(np.eye(col_tiles, dtype=np.float32), low)
    return fine, rows_low.astype(jnp.bfloat16), cols_low.astype(jnp.bfloat16)


def fold_sources(z_size, doubles):
    made = [[] for _ in range(doubles)]
    for z in range(z_size):
        for c in range(2):
            first = CHIP_PAIRS * z + 7 * c
            for p in range(PAIRS):
                pair = first + p
                block = p // 2 if first % 2 == 0 else ((p + 1) // 2) % 4
                lo = 64 * (pair % 2)
                hi = lo + 64
                if c == 0 and p == 7:
                    hi -= 32
                if c == 1 and p == 0:
                    lo += 32
                made[pair // 2].append((c, z, block, lo, hi))
    joined = []
    for parts in made:
        blocks = {}
        for c, z, block, lo, hi in parts:
            old = blocks.get((c, z, block), (lo, hi))
            blocks[c, z, block] = (min(old[0], lo), max(old[1], hi))
        joined.append([(k, v) for k, v in blocks.items()])
    return joined


def kernel(
    Y, Z, scale,
    at_ref, cot_ref, xt_ref, w_ref, mom_ref, chosen_ref, counts_ref, fine_ref, rl_ref, cl_ref,
    values_ref, newm_ref,
    a_own, c_own, a_sib, c_sib, xt, xr, low_in, wall, wmat, wfold, mfold, wpair, u0, grad, prod, own,
    send_p, send_m, got_p, got_m, pack, ys, xs, sall, smat, base, nfold,
    load_sem, a_send, a_recv, c_send, c_recv,
    rp_send, rp_recv, rm_send, rm_recv,
    wz_send, wz_recv, wy_send, wy_recv, wx_send, wx_recv, wc_send, wc_recv,
    sz_send, sz_recv, sy_send, sy_recv, sx_send, sx_recv, sc_send, sc_recv,
    ry_send, ry_recv, rx_send, rx_recv, out_sem,
):
    H = Z // 2
    ZS = Z // XS
    UP = PAIRS // Y
    D = at_ref.shape[0]
    RT = D // TILE
    KB = xr.shape[1] // 256
    replica, tok = lax.axis_index("replica"), lax.axis_index("tok")
    y, x = replica // XS, replica % XS
    z, c = tok // 2, tok % 2
    me = (replica, tok)
    sib = (replica, z * 2 + (1 - c))

    def at_z(o):
        return (replica, ((z + o) % Z) * 2 + c)

    def at_y(o):
        return (((y + o) % Y) * XS + x, tok)

    def at_x(o):
        return (y * XS + (x + o) % XS, tok)

    def rc(src, dst, ss, rs, dev):
        return pltpu.make_async_remote_copy(
            src_ref=src, dst_ref=dst, send_sem=ss, recv_sem=rs,
            device_id=dev, device_id_type=pl.DeviceIdType.MESH)

    def dot(a, b):
        return lax.dot_general(a, b, (((1,), (0,)), ((), ())), preferred_element_type=F32)

    def dot_fine(a, b):
        return lax.dot_general(a, b, (((1,), (0,)), ((), ())), preferred_element_type=F32,
                               precision=lax.Precision.HIGHEST)

    loads = [
        pltpu.make_async_copy(cot_ref, c_own, load_sem.at[0]),
        pltpu.make_async_copy(at_ref, a_own, load_sem.at[1]),
        pltpu.make_async_copy(w_ref, wfold.at[pl.ds(1, 15)], load_sem.at[2]),
        pltpu.make_async_copy(mom_ref, mfold.at[pl.ds(1, 15)], load_sem.at[3]),
        pltpu.make_async_copy(xt_ref, xt.at[pl.ds(0, D)], load_sem.at[4]),
    ]

    barrier = pltpu.get_barrier_semaphore()
    pl.semaphore_signal(barrier, inc=1, device_id=sib, device_id_type=pl.DeviceIdType.MESH)
    for o in range(1, Z):
        pl.semaphore_signal(barrier, inc=1, device_id=at_z(o), device_id_type=pl.DeviceIdType.MESH)
    for o in range(1, Y):
        pl.semaphore_signal(barrier, inc=1, device_id=at_y(o), device_id_type=pl.DeviceIdType.MESH)
    for o in range(1, XS):
        pl.semaphore_signal(barrier, inc=1, device_id=at_x(o), device_id_type=pl.DeviceIdType.MESH)
    for load in loads:
        load.start()

    lane = lax.broadcasted_iota(jnp.int32, (32, 128), 1)
    left = lane < 64

    wfold[0] = jnp.zeros((32, 128), BF16)
    wfold[16] = jnp.zeros((32, 128), BF16)
    mfold[0] = jnp.zeros((32, 128), F32)
    mfold[16] = jnp.zeros((32, 128), F32)
    got_p[0, 4:8] = jnp.zeros((4, TILE, 128), BF16)
    got_m[0, 0:4] = jnp.zeros((4, TILE, 128), BF16)
    if KB * 256 > D:
        xt[D:, :] = jnp.zeros((KB * 256 - D, xt.shape[1]), BF16)
        wmat[D:, :] = jnp.zeros((KB * 256 - D, wmat.shape[1]), BF16)
        smat[D // 2:, :] = jnp.zeros((KB * 128 - D // 2, smat.shape[1]), BF16)

    pl.semaphore_wait(barrier, Z + Y + XS - 2)

    def row_start(e, core):
        dest = (z + e) % Z
        return jnp.minimum((CHIP_PAIRS * dest + 7 * core) // 4, RT - 3) * TILE

    def a_copy(e):
        rows = pl.ds(pl.multiple_of(row_start(e, 1 - c), TILE), 3 * TILE)
        return rc(at_ref.at[rows], a_sib.at[e], a_send.at[e], a_recv.at[e], sib)

    c_copy = rc(cot_ref, c_sib, c_send, c_recv, sib)
    c_copy.start()
    a_copy(H).start()

    @pl.loop(1, H)
    def _(s):
        a_copy(H - s).start()
        a_copy(H + s).start()

    a_copy(0).start()

    class Spread:
        def __init__(self, buf, zs_, zr, ys_, yr, xs_, xr_, cs, cr):
            self.buf, self.zs, self.zr, self.ys, self.yr = buf, zs_, zr, ys_, yr
            self.xs, self.xr, self.cs, self.cr = xs_, xr_, cs, cr

        def mine(self):
            return self.buf.at[c, x, pl.ds(UP * y, UP)]

        def z_copy(self, o):
            part = self.mine().at[:, z // XS]
            return rc(part, part, self.zs.at[o - 1], self.zr.at[z // XS], at_z(o))

        def start_z(self):
            @pl.when(z % XS == x)
            def _():
                @pl.loop(1, Z)
                def _(o):
                    self.z_copy(o).start()

        def wait_z(self):
            @pl.loop(0, ZS)
            def _(k):
                @pl.when(z != x + XS * k)
                def _():
                    part = self.mine().at[:, k]
                    rc(part, part, self.zs.at[0], self.zr.at[k], at_z(1)).wait_recv()

        def y_copy(self, o):
            return rc(self.mine(), self.mine(), self.ys.at[o - 1], self.yr.at[o - 1], at_y(o))

        def start_y(self):
            @pl.loop(1, Y)
            def _(o):
                self.y_copy(o).start()

        def wait_y(self):
            @pl.loop(1, Y)
            def _(o):
                part = self.buf.at[c, x, pl.ds(UP * ((y + Y - o) % Y), UP)]
                rc(part, part, self.ys.at[o - 1], self.yr.at[o - 1], at_y(1)).wait_recv()

        def x_copy(self, k):
            if k < 2:
                part = self.buf.at[c, x]
            else:
                near = (x + XS - 1) % XS if k == 2 else (x + 1) % XS
                part = self.buf.at[c, near, pl.ds(0 if k == 2 else 4, 4)]
            return rc(part, part, self.xs.at[k], self.xr.at[k], at_x(1 if k % 2 == 0 else XS - 1))

        def c_copy(self, k):
            part = self.buf.at[c, (x + k) % XS]
            return rc(part, part, self.cs.at[k], self.cr.at[k], sib)

        def start_x(self):
            self.x_copy(0).start()
            self.x_copy(1).start()
            self.c_copy(0).start()

        def forward_x(self):
            from_left = self.buf.at[c, (x + XS - 1) % XS]
            rc(from_left, from_left, self.xs.at[0], self.xr.at[0], at_x(1)).wait_recv()
            self.x_copy(2).start()
            self.c_copy(3).start()
            from_right = self.buf.at[c, (x + 1) % XS]
            rc(from_right, from_right, self.xs.at[1], self.xr.at[1], at_x(1)).wait_recv()
            self.x_copy(3).start()
            self.c_copy(1).start()

        def finish_x(self):
            far = (x + 2) % XS
            for k in (2, 3):
                part = self.buf.at[c, far, pl.ds(0 if k == 2 else 4, 4)]
                rc(part, part, self.xs.at[k], self.xr.at[k], at_x(1)).wait_recv()
            self.c_copy(2).start()

        def wait_core(self):
            for k in range(XS):
                part = self.buf.at[1 - c, (x + k) % XS]
                rc(part, part, self.cs.at[k], self.cr.at[k], sib).wait_recv()

        def wait_sends(self):
            @pl.when(z % XS == x)
            def _():
                @pl.loop(1, Z)
                def _(o):
                    self.z_copy(o).wait_send()

            @pl.loop(1, Y)
            def _(o):
                self.y_copy(o).wait_send()

            for k in range(4):
                self.x_copy(k).wait_send()
            for k in range(XS):
                self.c_copy(k).wait_send()

    wide = Spread(wall, wz_send, wz_recv, wy_send, wy_recv, wx_send, wx_recv, wc_send, wc_recv)
    quads = Spread(sall, sz_send, sz_recv, sy_send, sy_recv, sx_send, sx_recv, sc_send, sc_recv)

    def unfold(fold_ref, p):
        first = fold_ref[1 + 2 * p - c].astype(F32)
        second = fold_ref[2 + 2 * p - c].astype(F32)
        even = jnp.where(left, first, pltpu.roll(second, 64, 1))
        odd = jnp.where(left, pltpu.roll(first, 64, 1), second)
        return even, odd

    loads[2].wait()

    @pl.when(z % XS == x)
    def _():
        for k in range(UP):
            even, odd = unfold(wfold, UP * y + k)
            wpair[pl.ds(0, 32, stride=2), :] = even
            wpair[pl.ds(1, 32, stride=2), :] = odd
            wall[c, x, UP * y + k, z // XS] = wpair[...].astype(BF16)

    wide.start_z()

    loads[0].wait()
    loads[1].wait()
    rc(c_sib, c_sib, c_send, c_recv, sib).wait_recv()

    def partial(e, slot):
        rc(a_sib.at[e], a_sib.at[e], a_send.at[e], a_recv.at[e], sib).wait_recv()
        start = row_start(e, c)
        rows = pl.ds(pl.multiple_of(start, TILE), 3 * TILE)
        total = dot(a_own[rows, :], c_own[...]) + dot(a_sib[e], c_sib[...])
        total = total * scale
        for j in range(4):
            prod[j] = total[:, 128 * j:128 * j + 128]
        first = CHIP_PAIRS * ((z + e) % Z) + 7 * c
        for p in range(PAIRS):
            pair = first + p
            row = pl.multiple_of((pair // 4) * TILE - start, TILE)
            own[slot, p] = prod[pair % 4, pl.ds(row, TILE), :]

    def p_copy(s, h):
        return rc(send_p.at[s, pl.ds(4 * h, 4)], got_p.at[s, pl.ds(4 * h, 4)],
                  rp_send.at[s, h], rp_recv.at[s, h], at_z(1))

    def m_copy(s, h):
        return rc(send_m.at[s, pl.ds(4 * h, 4)], got_m.at[s, pl.ds(4 * h, 4)],
                  rm_send.at[s, h], rm_recv.at[s, h], at_z(Z - 1))

    partial(H, 0)
    send_p[0, 0:4] = own[0, 0:4].astype(BF16)
    p_copy(0, 0).start()
    send_m[0, 4:8] = own[0, 4:8].astype(BF16)
    m_copy(0, 1).start()

    @pl.loop(1, H)
    def _(s):
        partial(H - s, 0)
        partial(H + s, 1)
        for step in range(2):
            hp, hm = step, 1 - step
            if step == 0:
                p_copy(s - 1, hp).wait_recv()
            else:
                @pl.when(s > 1)
                def _():
                    p_copy(s - 1, hp).wait_recv()
            part = own[0, 4 * hp:4 * hp + 4] + got_p[s - 1, 4 * hp:4 * hp + 4].astype(F32)
            send_p[s, 4 * hp:4 * hp + 4] = part.astype(BF16)
            p_copy(s, hp).start()
            if step == 0:
                m_copy(s - 1, hm).wait_recv()
            else:
                @pl.when(s > 1)
                def _():
                    m_copy(s - 1, hm).wait_recv()
            part = own[1, 4 * hm:4 * hm + 4] + got_m[s - 1, 4 * hm:4 * hm + 4].astype(F32)
            send_m[s, 4 * hm:4 * hm + 4] = part.astype(BF16)
            m_copy(s, hm).start()

        @pl.when(s == 1)
        def _():
            wide.wait_z()
            wide.start_y()

        @pl.when(s == min(3, H - 1))
        def _():
            wide.wait_y()
            wide.start_x()

    partial(0, 0)

    loads[3].wait()
    for p in range(PAIRS):
        even, odd = unfold(mfold, p)
        u0[p, pl.ds(0, 32, stride=2), :] = even * momentum_decay
        u0[p, pl.ds(1, 32, stride=2), :] = odd * momentum_decay
    for p in range(PAIRS):
        own[0, p] = own[0, p] + u0[p]

    shape = (PAIRS * KEEP, 128)
    number = 2 * (lax.broadcasted_iota(jnp.int32, shape, 0) // KEEP) - c
    number = number + (lax.broadcasted_iota(jnp.int32, shape, 1) // KEEP) % 2
    keep = jnp.zeros(shape, F32)
    for s in range(8):
        listed = jnp.where(s < counts_ref[0], chosen_ref[s], -5)
        keep = jnp.where(number == listed, 1.0, keep)

    for h in range(2):
        p_copy(H - 1, h).wait_recv()
        m_copy(H - 1, h).wait_recv()
    for p in range(PAIRS):
        grad[p] = own[0, p] + (got_p[H - 1, p].astype(F32) + got_m[H - 1, p].astype(F32))

    low = fine_ref[0:32, 0:64]
    side = dot_fine(low, jnp.concatenate([grad[p] for p in range(PAIRS)], axis=1))
    side = jnp.concatenate([side[:, 128 * p:128 * p + 128] for p in range(PAIRS)], axis=0)
    quad = dot_fine(side, fine_ref[96:224, :])
    quad = jnp.where(keep > 0.5, quad, 0.0).astype(BF16).astype(F32)
    odd_first = ((z + c) % 2) == 1
    for d in range(4):
        blocks = [quad[32 * p:32 * p + 32] for p in range(PAIRS)]
        plain = jnp.where(left, blocks[2 * d], blocks[2 * d + 1])
        turned = jnp.where(left, blocks[(2 * d + 7) % 8], blocks[2 * d])
        block = jnp.where(odd_first, turned, plain).astype(BF16)
        pack[2 * d] = block[0:16]
        pack[2 * d + 1] = block[16:32]

    def ry_copy(o):
        return rc(pack.at[pl.ds(UP * ((y + o) % Y), UP)], ys.at[o - 1],
                  ry_send.at[o - 1], ry_recv.at[o - 1], at_y(o))

    @pl.loop(1, Y)
    def _(o):
        ry_copy(o).start()

    wide.forward_x()

    @pl.loop(1, Y)
    def _(o):
        ry_copy(o).wait_recv()

    total = pack[pl.ds(UP * y, UP)].astype(F32)
    for o in range(1, Y):
        total = total + ys[o - 1].astype(F32)
    xs[0] = total

    def rx_copy(o):
        return rc(xs.at[0], xs.at[o], rx_send.at[o - 1], rx_recv.at[o - 1], at_x(o))

    for o in range(1, XS):
        rx_copy(o).start()

    quad_side = dot_fine(quad[:, 0:64], fine_ref[224:288, :])
    quad_side = jnp.concatenate([quad_side[32 * p:32 * p + 32] for p in range(PAIRS)], axis=1)
    shift = dot_fine(fine_ref[32:96, 0:32], quad_side)
    for p in range(PAIRS):
        grad[p] = grad[p] - shift[:, 128 * p:128 * p + 128]

    for o in range(1, XS):
        rx_copy(o).wait_recv()
    total = (xs[0] + xs[2]) + (xs[1] + xs[3])

    @pl.when(z % XS == x)
    def _():
        for k in range(UP):
            sall[c, x, UP * y + k, z // XS] = total[k].astype(BF16)

    quads.start_z()

    for p in range(PAIRS):
        even = grad[p, pl.ds(0, 32, stride=2), :]
        odd = grad[p, pl.ds(1, 32, stride=2), :]
        nfold[1 + 2 * p - c] = jnp.where(left, even, pltpu.roll(odd, 64, 1))
        nfold[2 + 2 * p - c] = jnp.where(left, pltpu.roll(even, 64, 1), odd)
    out_copy = pltpu.make_async_copy(nfold.at[pl.ds(1, 15)], newm_ref, out_sem)
    out_copy.start()

    quads.wait_z()
    quads.start_y()
    loads[4].wait()
    wide.finish_x()

    @pl.loop(0, KB)
    def _(k):
        rows = pl.ds(pl.multiple_of(256 * k, 256), 256)
        xr[:, rows] = xt[rows, :].T

    quads.wait_y()
    quads.start_x()

    @pl.loop(0, KB)
    def _(k):
        rows = pl.ds(pl.multiple_of(256 * k, 256), 256)
        low_in[:, pl.ds(pl.multiple_of(128 * k, 128), 128)] = dot(xr[:, rows], rl_ref[...]).astype(BF16)

    wide.wait_core()
    left64 = lax.broadcasted_iota(jnp.int32, (TILE, 128), 1) < 64
    for zz in range(Z):
        for p in range(CHIP_PAIRS):
            pair = CHIP_PAIRS * zz + p
            core, slot = (0, p) if p < 8 else (1, p - 7)
            block = wall[core, zz % XS, slot, zz // XS]
            if p == 7:
                block = jnp.where(left64, block, wall[1, zz % XS, 0, zz // XS])
            wmat[TILE * (pair // 4):TILE * (pair // 4) + TILE,
                 128 * (pair % 4):128 * (pair % 4) + 128] = block

    quads.forward_x()
    base[...] = jnp.zeros(base.shape, F32)

    @pl.loop(0, KB)
    def _(k):
        rows = pl.ds(pl.multiple_of(256 * k, 256), 256)
        base[...] += dot(xr[:, rows], wmat[rows, :])

    quads.finish_x()
    quads.wait_core()

    lane16 = lax.broadcasted_iota(jnp.int32, (16, 128), 1)
    for n, parts in enumerate(fold_sources(Z, D * 2 // 64)):
        for half in range(2):
            block = None
            for (core, zz, d), (lo, hi) in parts:
                part = sall[core, zz % XS, 2 * d + half, zz // XS]
                if block is None:
                    block = part
                else:
                    block = jnp.where((lane16 >= lo) & (lane16 < hi), part, block)
            row = 32 * (n // 2) + 16 * half
            smat[row:row + 16, 128 * (n % 2):128 * (n % 2) + 128] = block

    late = dot(low_in[...], smat[...]) * step_size
    values_ref[...] = (base[...] - dot(late.astype(BF16), cl_ref[...])).astype(BF16)

    out_copy.wait()
    c_copy.wait_send()

    @pl.loop(0, Z)
    def _(e):
        a_copy(e).wait_send()

    p_copy(0, 0).wait_send()
    m_copy(0, 1).wait_send()

    @pl.loop(1, H)
    def _(s):
        for h in range(2):
            p_copy(s, h).wait_send()
            m_copy(s, h).wait_send()

    @pl.loop(1, Y)
    def _(o):
        ry_copy(o).wait_send()

    for o in range(1, XS):
        rx_copy(o).wait_send()
    wide.wait_sends()
    quads.wait_sends()


def local(Y, Z, activations, cotangent, next_inputs, weight_tiles, momentum, chosen, counts):
    tokens, depth = activations.shape
    width = cotangent.shape[1]
    scale = 1.0 / math.sqrt(tokens * 2 * Z)
    H, ZS, UP = Z // 2, Z // XS, PAIRS // Y
    KB = -(-depth // 256)
    fine, rows_low, cols_low = tables(width // TILE)
    hbm = pl.BlockSpec(memory_space=pl.ANY)
    vmem = pl.BlockSpec(memory_space=pltpu.VMEM)
    smem = pl.BlockSpec(memory_space=pltpu.SMEM)
    dma = pltpu.SemaphoreType.DMA
    spread_sems = [dma((Z - 1,)), dma((ZS,)), dma((Y,)), dma((Y,)), dma((4,)), dma((4,)), dma((4,)), dma((4,))]
    pairs = (PAIRS, TILE, 128)
    scratch = [
        pltpu.VMEM((depth, tokens), BF16),
        pltpu.VMEM((tokens, width), BF16),
        pltpu.VMEM((Z, 3 * TILE, tokens), BF16),
        pltpu.VMEM((tokens, width), BF16),
        pltpu.VMEM((KB * 256, tokens), BF16),
        pltpu.VMEM((tokens, KB * 256), BF16),
        pltpu.VMEM((tokens, KB * 128), BF16),
        pltpu.VMEM((2, XS, PAIRS, ZS, TILE, 128), BF16),
        pltpu.VMEM((KB * 256, width), BF16),
        pltpu.VMEM((17, 32, 128), BF16),
        pltpu.VMEM((17, 32, 128), F32),
        pltpu.VMEM((TILE, 128), F32),
        pltpu.VMEM(pairs, F32),
        pltpu.VMEM(pairs, F32),
        pltpu.VMEM((4, 3 * TILE, 128), F32),
        pltpu.VMEM((2,) + pairs, F32),
        pltpu.VMEM((H,) + pairs, BF16),
        pltpu.VMEM((H,) + pairs, BF16),
        pltpu.VMEM((H,) + pairs, BF16),
        pltpu.VMEM((H,) + pairs, BF16),
        pltpu.VMEM((8, 16, 128), BF16),
        pltpu.VMEM((Y, UP, 16, 128), BF16),
        pltpu.VMEM((XS, UP, 16, 128), F32),
        pltpu.VMEM((2, XS, PAIRS, ZS, 16, 128), BF16),
        pltpu.VMEM((KB * 128, width // 2), BF16),
        pltpu.VMEM((tokens, width), F32),
        pltpu.VMEM((17, 32, 128), F32),
        dma((5,)), dma((Z,)), dma((Z,)), dma(()), dma(()),
        dma((H, 2)), dma((H, 2)), dma((H, 2)), dma((H, 2)),
        *spread_sems, *spread_sems,
        dma((Y,)), dma((Y,)), dma((XS,)), dma((XS,)), dma(()),
    ]
    values, new_momentum = pl.pallas_call(
        functools.partial(kernel, Y, Z, scale),
        out_shape=(
            jax.ShapeDtypeStruct((tokens, width), BF16),
            jax.ShapeDtypeStruct((15, 32, 128), F32),
        ),
        in_specs=[hbm, hbm, hbm, hbm, hbm, smem, smem, vmem, vmem, vmem],
        out_specs=(vmem, hbm),
        scratch_shapes=scratch,
        compiler_params=pltpu.CompilerParams(
            collective_id=0, has_side_effects=True, vmem_limit_bytes=48 * 1024 * 1024),
        cost_estimate=pl.CostEstimate(
            flops=4 * tokens * depth * width, bytes_accessed=8 * tokens * depth, transcendentals=0),
    )(
        activations.T, cotangent, next_inputs.T, weight_tiles.reshape(15, 32, 128),
        momentum.reshape(15, 32, 128), chosen.reshape(8), counts.reshape(1),
        jnp.asarray(fine), jnp.asarray(rows_low), jnp.asarray(cols_low),
    )
    return values, new_momentum.reshape(1, 15, TILE * TILE)


def solution(mesh):
    Y, Z = mesh.shape["replica"] // XS, mesh.shape["tok"] // 2
    return jax.shard_map(
        functools.partial(local, Y, Z),
        mesh=mesh,
        in_specs=(
            P(("replica", "tok"), None),
            P(("replica", "tok"), None),
            P(("replica", "tok"), None),
            P("tok", None),
            P("replica", "tok", None),
            P("replica", "tok", None),
            P("replica", "tok"),
        ),
        out_specs=(P(("replica", "tok"), None), P("replica", "tok", None)),
        check_vma=False,
    )
```

time: 255 us -> 91.9 us (0.36)
  blocking collectives: 107 us -> 0 us
  Pallas kernels: 0 us -> 79.8 us
  waiting for transfers between devices: 72.2 us -> 0 us
  local copies, waits for them, and re-layouts: 41 us -> 10.3 us
  between operations: 16.2 us -> 1.31 us
  matrix products: 11.4 us -> 0 us
  starting transfers between devices: 4.33 us -> 0 us
    pallas_call x0 -> x1, Pallas kernels: none -> 79.8 us  [local(): pl.pallas_call(functools.partial(kernel, Y, Z, scale), out_shape=(jax.Sha...]
    all_gather x1 -> x0, waiting for transfers between devices: 72.2 us -> none  [local(): new_full = lax.all_gather(new_part, 'tok', axis=0, tiled=True)]
    unnamed x2 -> x0, blocking collectives: 71.4 us -> none
    all_gather x1 -> x0, blocking collectives: 35.6 us -> none  [local(): lax.all_gather(flat_quads, 'replica', axis=0, tiled=True)]
    convert_element_type x3 -> x0, local copies, waits for them, and re-layouts: 24.1 us -> none  [local(): tiled.astype(jnp.bfloat16)]
    dot_general x9 -> x0, matrix products: 11.4 us -> none  [the longest x1 4.42 us: forward(): jnp.einsum('tra,rcab->tcb', blocks, matrix, preferred_element_type=jnp.fl...]
    reshape x3 -> x1, local copies, waits for them, and re-layouts: 9.61 us -> 0.01 us  [local(): weight_tiles.reshape(15, 32, 128)]
    unnamed x2 -> x0, starting transfers between devices: 4.29 us -> none
  transfers between devices with their start and end apart: 3 -> 0, of which waited for: 1 -> 0; matrix products, arithmetic and copies ran while one was open for 2% -> 0% of each run, Pallas kernels for 0% -> 0%
where the time goes in v1:
time: 91.9 us; the launch traced here: 91.5 us
  Pallas kernels  79.8 us (87%)
  local copies, waits for them, and re-layouts  10.3 us (11%)
  between operations  1.31 us (1%)
    pallas_call x1, Pallas kernels, local(): pl.pallas_call(functools.partial(kernel, Y, Z, scale), out_shape=(jax.Sha...  79.8 us
    unnamed x19, local copies, waits for them, and re-layouts  10.3 us

profile of v1, /device:TPU:1, one launch (start us, length us, event | category | flops | bytes accessed | tf_op | source)
XLA Modules:
  0.0 91.5 jit_solution(3928878690674654241)
XLA Ops:
  1.3 0.9 %copy.14 = bf16[2,8,32,128]{3,2,1,0:T(8,128)(2,1)S(1)} copy(bf16[2,8,32,128]{3,1,2,0:T(8,128)(2,1)} %bitcast.16) | data formatting | bytes 262144
  2.2 0.0 copy-start
  2.2 1.4 %copy-done = bf16[256,2880]{0,1:T(8,128)(2,1)S(1)} copy-done((bf16[256,2880]{0,1:T(8,128)(2,1)S(1)}, bf16[256,2880]{0,1:T(8,128)(2,1)}, u32[]{:S(2)}) %copy-start) | copy-done | bytes 1474584
  3.6 0.0 copy-start.1
  3.6 1.4 %copy-done.1 = bf16[256,2880]{0,1:T(8,128)(2,1)S(1)} copy-done((bf16[256,2880]{0,1:T(8,128)(2,1)S(1)}, bf16[256,2880]{0,1:T(8,128)(2,1)}, u32[]{:S(2)}) %copy-start.1) | copy-done | bytes 1474584
  5.0 0.0 copy-start.2
  5.0 0.9 %copy-done.2 = bf16[256,512]{1,0:T(8,128)(2,1)S(1)} copy-done((bf16[256,512]{1,0:T(8,128)(2,1)S(1)}, bf16[256,512]{1,0:T(8,128)(2,1)}, u32[]{:S(2)}) %copy-start.2) | copy-done | bytes 262168
  5.9 0.0 copy-start.3
  5.9 0.9 %copy-done.3 = f32[1,15,4096]{2,0,1:T(1,128)S(1)} copy-done((f32[1,15,4096]{2,0,1:T(1,128)S(1)}, f32[1,15,4096]{2,0,1:T(1,128)}, u32[]{:S(2)}) %copy-start.3) | copy-done | bytes 245784
  6.9 0.0 copy-start.4
  6.9 0.7 copy-done.4
  7.5 0.0 copy-start.5
  7.5 0.9 %copy-done.5 = bf16[256,512]{1,0:T(8,128)(2,1)S(1)} copy-done((bf16[256,512]{1,0:T(8,128)(2,1)S(1)}, bf16[256,512]{1,0:T(8,128)(2,1)}, u32[]{:S(2)}) %copy-start.5) | copy-done | bytes 262168
  8.5 0.0 copy-start.6
  8.5 0.9 %copy-done.6 = f32[352,128]{1,0:T(8,128)S(1)} copy-done((f32[352,128]{1,0:T(8,128)S(1)}, f32[352,128]{1,0:T(8,128)}, u32[]{:S(2)}) %copy-start.6) | copy-done | bytes 180248
  9.4 0.0 copy-start.7
  9.4 0.8 copy-done.7
  10.2 79.8 %shard_map.113 = (bf16[256,512]{1,0:T(8,128)(2,1)S(1)}, f32[15,32,128]{2,1,0:T(8,128)S(1)}) custom-call(bf16[2880,256]{1,0:T(8,128)(2,1)S(1)} %bitcast.11, bf16[256,512]{1,0:T(8,128)(2,1)S(1)} %copy-done.2, bf16[2880,256]{1,0:T(8,128)(2,1)S(1)} %bitcast.12, bf16[15,32,128]{2,1,0:T(8,128)(2,1)S(1)} %slice.w_ref, f32[15,32,128]{2,1,0:T(8,128)S(1)} %bitcast.13, ...), custom_call_target="tpu_custom_call" | custom-call | flops 1509949440 | bytes 5898240 | tf_op jit(solution)/shard_map/pallas_call | solution.py:573
  90.1 0.7 copy.18
  90.8 0.7 copy.19
  (1 shorter events, 0.0 us)
Async XLA Ops:
  2.2 1.4 %copy-start = (bf16[256,2880]{0,1:T(8,128)(2,1)S(1)}, bf16[256,2880]{0,1:T(8,128)(2,1)}, u32[]{:S(2)}) copy-start(bf16[256,2880]{0,1:T(8,128)(2,1)} %param.10) | copy-start | bytes 4423684
  3.6 1.4 %copy-start.1 = (bf16[256,2880]{0,1:T(8,128)(2,1)S(1)}, bf16[256,2880]{0,1:T(8,128)(2,1)}, u32[]{:S(2)}) copy-start(bf16[256,2880]{0,1:T(8,128)(2,1)} %param.12) | copy-start | bytes 4423684
  5.0 0.9 %copy-start.2 = (bf16[256,512]{1,0:T(8,128)(2,1)S(1)}, bf16[256,512]{1,0:T(8,128)(2,1)}, u32[]{:S(2)}) copy-start(bf16[256,512]{1,0:T(8,128)(2,1)} %cot_ref.1) | copy-start | bytes 786436
  5.9 0.9 %copy-start.3 = (f32[1,15,4096]{2,0,1:T(1,128)S(1)}, f32[1,15,4096]{2,0,1:T(1,128)}, u32[]{:S(2)}) copy-start(f32[1,15,4096]{2,0,1:T(1,128)} %param.14) | copy-start | bytes 737284
  6.9 0.7 copy-start.4
  7.5 0.9 %copy-start.5 = (bf16[256,512]{1,0:T(8,128)(2,1)S(1)}, bf16[256,512]{1,0:T(8,128)(2,1)}, u32[]{:S(2)}) copy-start(bf16[256,512]{1,0:T(8,128)(2,1)} %constant.8.clone.cl_ref) | copy-start | bytes 786436
  8.5 0.9 %copy-start.6 = (f32[352,128]{1,0:T(8,128)S(1)}, f32[352,128]{1,0:T(8,128)}, u32[]{:S(2)}) copy-start(f32[352,128]{1,0:T(8,128)} %constant.6.clone.fine_ref) | copy-start | bytes 540676
  9.4 0.8 copy-start.7

commit v2 on v1

--- a/solution.py
+++ b/solution.py
@@ -30,18 +30,28 @@
     return (cosines * factor).astype(np.float32)
 
 
+def split(values):
+    high = values.astype(jnp.bfloat16)
+    return high, (values - high.astype(jnp.float32)).astype(jnp.bfloat16)
+
+
 def tables(col_tiles):
     low = cosine_table()
-    fine = np.zeros((352, 128), np.float32)
-    fine[0:32, 0:64] = low
-    fine[32:96, 0:32] = low.T
+    high_part, low_part = (np.asarray(v, np.float32) for v in split(low))
     two = np.kron(np.eye(2, dtype=np.float32), low.T)
-    fine[96:224, 0:64] = two
-    fine[96:224, 64:128] = two
-    fine[224:288, :] = two.T
+    twice = np.concatenate([two, two], axis=1)
+    back = np.concatenate([two.T, np.zeros((64, 128), np.float32)], axis=0)
+    fine = np.zeros((768, 128), np.float32)
+    fine[0:32, 0:64] = fine[0:32, 64:128] = high_part
+    fine[32:64, 0:64] = fine[32:64, 64:128] = low_part
+    fine[64:128, 0:32] = fine[64:128, 32:64] = high_part.T
+    fine[64:128, 64:96] = low_part.T
+    fine[128:256], fine[384:512] = (np.asarray(v, np.float32) for v in split(twice))
+    fine[256:384] = fine[128:256]
+    fine[512:640], fine[640:768] = (np.asarray(v, np.float32) for v in split(back))
     rows_low = np.kron(np.eye(4, dtype=np.float32), low.T)
     cols_low = np.kron(np.eye(col_tiles, dtype=np.float32), low)
-    return fine, rows_low.astype(jnp.bfloat16), cols_low.astype(jnp.bfloat16)
+    return fine.astype(jnp.bfloat16), rows_low.astype(jnp.bfloat16), cols_low.astype(jnp.bfloat16)
 
 
 def fold_sources(z_size, doubles):
@@ -71,10 +81,11 @@
 
 def kernel(
     Y, Z, scale,
-    at_ref, cot_ref, xt_ref, w_ref, mom_ref, chosen_ref, counts_ref, fine_ref, rl_ref, cl_ref,
+    at_ref, cot_ref, xt_ref, w_ref, mom_ref, chosen_in, counts_in, fine_in, rl_in, cl_in,
     values_ref, newm_ref,
-    a_own, c_own, a_sib, c_sib, xt, xr, low_in, wall, wmat, wfold, mfold, wpair, u0, grad, prod, own,
+    a_own, c_own, a_sib, c_sib, xt, xr, low_in, wall, wmat, wfull, wfold, mfold, wpair, u0, grad, prod, own,
     send_p, send_m, got_p, got_m, pack, ys, xs, sall, smat, base, nfold,
+    fine_ref, rl_ref, cl_ref, chosen_ref, counts_ref,
     load_sem, a_send, a_recv, c_send, c_recv,
     rp_send, rp_recv, rm_send, rm_recv,
     wz_send, wz_recv, wy_send, wy_recv, wx_send, wx_recv, wc_send, wc_recv,
@@ -110,16 +121,17 @@
     def dot(a, b):
         return lax.dot_general(a, b, (((1,), (0,)), ((), ())), preferred_element_type=F32)
 
-    def dot_fine(a, b):
-        return lax.dot_general(a, b, (((1,), (0,)), ((), ())), preferred_element_type=F32,
-                               precision=lax.Precision.HIGHEST)
-
     loads = [
         pltpu.make_async_copy(cot_ref, c_own, load_sem.at[0]),
         pltpu.make_async_copy(at_ref, a_own, load_sem.at[1]),
-        pltpu.make_async_copy(w_ref, wfold.at[pl.ds(1, 15)], load_sem.at[2]),
+        pltpu.make_async_copy(w_ref, wfull, load_sem.at[2]),
         pltpu.make_async_copy(mom_ref, mfold.at[pl.ds(1, 15)], load_sem.at[3]),
         pltpu.make_async_copy(xt_ref, xt.at[pl.ds(0, D)], load_sem.at[4]),
+        pltpu.make_async_copy(fine_in, fine_ref, load_sem.at[5]),
+        pltpu.make_async_copy(rl_in, rl_ref, load_sem.at[6]),
+        pltpu.make_async_copy(cl_in, cl_ref, load_sem.at[7]),
+        pltpu.make_async_copy(chosen_in, chosen_ref, load_sem.at[8]),
+        pltpu.make_async_copy(counts_in, counts_ref, load_sem.at[9]),
     ]
 
     barrier = pltpu.get_barrier_semaphore()
@@ -136,8 +148,6 @@
     lane = lax.broadcasted_iota(jnp.int32, (32, 128), 1)
     left = lane < 64
 
-    wfold[0] = jnp.zeros((32, 128), BF16)
-    wfold[16] = jnp.zeros((32, 128), BF16)
     mfold[0] = jnp.zeros((32, 128), F32)
     mfold[16] = jnp.zeros((32, 128), F32)
     got_p[0, 4:8] = jnp.zeros((4, TILE, 128), BF16)
@@ -267,9 +277,7 @@
     wide = Spread(wall, wz_send, wz_recv, wy_send, wy_recv, wx_send, wx_recv, wc_send, wc_recv)
     quads = Spread(sall, sz_send, sz_recv, sy_send, sy_recv, sx_send, sx_recv, sc_send, sc_recv)
 
-    def unfold(fold_ref, p):
-        first = fold_ref[1 + 2 * p - c].astype(F32)
-        second = fold_ref[2 + 2 * p - c].astype(F32)
+    def unfold(first, second):
         even = jnp.where(left, first, pltpu.roll(second, 64, 1))
         odd = jnp.where(left, pltpu.roll(first, 64, 1), second)
         return even, odd
@@ -279,7 +287,14 @@
     @pl.when(z % XS == x)
     def _():
         for k in range(UP):
-            even, odd = unfold(wfold, UP * y + k)
+            number = 2 * (UP * y + k) - c
+            rows = lax.broadcasted_iota(jnp.int32, (15, 4096), 0)
+            for tile in range(2):
+                only = jnp.where(rows == number + tile, wfull[...].astype(F32), 0.0)
+                only = jnp.sum(only, axis=0, keepdims=True)
+                for r in range(32):
+                    wfold[tile, r:r + 1, :] = only[:, 128 * r:128 * r + 128]
+            even, odd = unfold(wfold[0], wfold[1])
             wpair[pl.ds(0, 32, stride=2), :] = even
             wpair[pl.ds(1, 32, stride=2), :] = odd
             wall[c, x, UP * y + k, z // XS] = wpair[...].astype(BF16)
@@ -317,70 +332,73 @@
     p_copy(0, 0).start()
     send_m[0, 4:8] = own[0, 4:8].astype(BF16)
     m_copy(0, 1).start()
+    wide.wait_z()
+    wide.start_y()
+    partial(H - 1, 2)
+    partial(H + 1, 3)
 
     @pl.loop(1, H)
     def _(s):
-        partial(H - s, 0)
-        partial(H + s, 1)
-        for step in range(2):
-            hp, hm = step, 1 - step
-            if step == 0:
-                p_copy(s - 1, hp).wait_recv()
-            else:
-                @pl.when(s > 1)
-                def _():
-                    p_copy(s - 1, hp).wait_recv()
-            part = own[0, 4 * hp:4 * hp + 4] + got_p[s - 1, 4 * hp:4 * hp + 4].astype(F32)
-            send_p[s, 4 * hp:4 * hp + 4] = part.astype(BF16)
-            p_copy(s, hp).start()
-            if step == 0:
-                m_copy(s - 1, hm).wait_recv()
-            else:
-                @pl.when(s > 1)
-                def _():
-                    m_copy(s - 1, hm).wait_recv()
-            part = own[1, 4 * hm:4 * hm + 4] + got_m[s - 1, 4 * hm:4 * hm + 4].astype(F32)
-            send_m[s, 4 * hm:4 * hm + 4] = part.astype(BF16)
-            m_copy(s, hm).start()
-
-        @pl.when(s == 1)
+        now, later = 2 * (s % 2), 2 * ((s + 1) % 2)
+
+        def pass_on(copy, got, send, slot, h, first):
+            @pl.when(jnp.logical_or(s > 1, first))
+            def _():
+                copy(s - 1, h).wait_recv()
+
+            part = own[slot, 4 * h:4 * h + 4] + got[s - 1, 4 * h:4 * h + 4].astype(F32)
+            send[s, 4 * h:4 * h + 4] = part.astype(BF16)
+            copy(s, h).start()
+
+        pass_on(p_copy, got_p, send_p, now, 0, True)
+        pass_on(m_copy, got_m, send_m, now + 1, 1, True)
+        partial(H - 1 - s, later)
+        pass_on(p_copy, got_p, send_p, now, 1, False)
+        pass_on(m_copy, got_m, send_m, now + 1, 0, False)
+
+        @pl.when(s < H - 1)
         def _():
-            wide.wait_z()
-            wide.start_y()
-
-        @pl.when(s == min(3, H - 1))
+            partial(H + 1 + s, later + 1)
+
+        @pl.when(s == min(4, H - 1))
         def _():
             wide.wait_y()
             wide.start_x()
 
-    partial(0, 0)
+    last = 2 * (H % 2)
 
     loads[3].wait()
+    loads[5].wait()
+    loads[8].wait()
+    loads[9].wait()
     for p in range(PAIRS):
-        even, odd = unfold(mfold, p)
+        even, odd = unfold(mfold[1 + 2 * p - c], mfold[2 + 2 * p - c])
         u0[p, pl.ds(0, 32, stride=2), :] = even * momentum_decay
         u0[p, pl.ds(1, 32, stride=2), :] = odd * momentum_decay
     for p in range(PAIRS):
-        own[0, p] = own[0, p] + u0[p]
+        u0[p] = own[last, p] + u0[p]
+    high, rest = split(jnp.concatenate([u0[p] for p in range(PAIRS)], axis=1))
+    side_own = dot(fine_ref[0:64, 0:64], high)
+    side_own = side_own[0:32] + side_own[32:64] + dot(fine_ref[0:32, 0:64], rest)
 
     shape = (PAIRS * KEEP, 128)
     number = 2 * (lax.broadcasted_iota(jnp.int32, shape, 0) // KEEP) - c
     number = number + (lax.broadcasted_iota(jnp.int32, shape, 1) // KEEP) % 2
     keep = jnp.zeros(shape, F32)
     for s in range(8):
-        listed = jnp.where(s < counts_ref[0], chosen_ref[s], -5)
+        listed = jnp.where(s < counts_ref[0, 0], chosen_ref[0, s], -5)
         keep = jnp.where(number == listed, 1.0, keep)
 
     for h in range(2):
         p_copy(H - 1, h).wait_recv()
         m_copy(H - 1, h).wait_recv()
-    for p in range(PAIRS):
-        grad[p] = own[0, p] + (got_p[H - 1, p].astype(F32) + got_m[H - 1, p].astype(F32))
-
-    low = fine_ref[0:32, 0:64]
-    side = dot_fine(low, jnp.concatenate([grad[p] for p in range(PAIRS)], axis=1))
+    arrived = jnp.concatenate(
+        [jnp.concatenate([got[H - 1, p] for p in range(PAIRS)], axis=1) for got in (got_p, got_m)], axis=0)
+    side = dot(fine_ref[0:64, :], arrived)
+    side = side_own + (side[0:32] + side[32:64])
     side = jnp.concatenate([side[:, 128 * p:128 * p + 128] for p in range(PAIRS)], axis=0)
-    quad = dot_fine(side, fine_ref[96:224, :])
+    high, rest = split(side)
+    quad = dot(jnp.concatenate([high, rest, high], axis=1), fine_ref[128:512, :])
     quad = jnp.where(keep > 0.5, quad, 0.0).astype(BF16).astype(F32)
     odd_first = ((z + c) % 2) == 1
     for d in range(4):
@@ -416,11 +434,14 @@
     for o in range(1, XS):
         rx_copy(o).start()
 
-    quad_side = dot_fine(quad[:, 0:64], fine_ref[224:288, :])
+    exact = quad.astype(BF16)
+    quad_side = dot(jnp.concatenate([exact, exact], axis=1), fine_ref[512:768, :])
     quad_side = jnp.concatenate([quad_side[32 * p:32 * p + 32] for p in range(PAIRS)], axis=1)
-    shift = dot_fine(fine_ref[32:96, 0:32], quad_side)
+    high, rest = split(quad_side)
+    shift = dot(fine_ref[64:128, 0:96], jnp.concatenate([high, rest, high], axis=0))
     for p in range(PAIRS):
-        grad[p] = grad[p] - shift[:, 128 * p:128 * p + 128]
+        got = got_p[H - 1, p].astype(F32) + got_m[H - 1, p].astype(F32)
+        grad[p] = (u0[p] + got) - shift[:, 128 * p:128 * p + 128]
 
     for o in range(1, XS):
         rx_copy(o).wait_recv()
@@ -444,6 +465,8 @@
     quads.wait_z()
     quads.start_y()
     loads[4].wait()
+    loads[6].wait()
+    loads[7].wait()
     wide.finish_x()
 
     @pl.loop(0, KB)
@@ -533,7 +556,6 @@
     fine, rows_low, cols_low = tables(width // TILE)
     hbm = pl.BlockSpec(memory_space=pl.ANY)
     vmem = pl.BlockSpec(memory_space=pltpu.VMEM)
-    smem = pl.BlockSpec(memory_space=pltpu.SMEM)
     dma = pltpu.SemaphoreType.DMA
     spread_sems = [dma((Z - 1,)), dma((ZS,)), dma((Y,)), dma((Y,)), dma((4,)), dma((4,)), dma((4,)), dma((4,))]
     pairs = (PAIRS, TILE, 128)
@@ -547,13 +569,14 @@
         pltpu.VMEM((tokens, KB * 128), BF16),
         pltpu.VMEM((2, XS, PAIRS, ZS, TILE, 128), BF16),
         pltpu.VMEM((KB * 256, width), BF16),
-        pltpu.VMEM((17, 32, 128), BF16),
+        pltpu.VMEM((15, TILE * TILE), BF16),
+        pltpu.VMEM((2, 32, 128), F32),
         pltpu.VMEM((17, 32, 128), F32),
         pltpu.VMEM((TILE, 128), F32),
         pltpu.VMEM(pairs, F32),
         pltpu.VMEM(pairs, F32),
         pltpu.VMEM((4, 3 * TILE, 128), F32),
-        pltpu.VMEM((2,) + pairs, F32),
+        pltpu.VMEM((4,) + pairs, F32),
         pltpu.VMEM((H,) + pairs, BF16),
         pltpu.VMEM((H,) + pairs, BF16),
         pltpu.VMEM((H,) + pairs, BF16),
@@ -565,7 +588,12 @@
         pltpu.VMEM((KB * 128, width // 2), BF16),
         pltpu.VMEM((tokens, width), F32),
         pltpu.VMEM((17, 32, 128), F32),
-        dma((5,)), dma((Z,)), dma((Z,)), dma(()), dma(()),
+        pltpu.VMEM(fine.shape, BF16),
+        pltpu.VMEM(rows_low.shape, BF16),
+        pltpu.VMEM(cols_low.shape, BF16),
+        pltpu.SMEM((1, 8), jnp.int32),
+        pltpu.SMEM((1, 1), jnp.int32),
+        dma((10,)), dma((Z,)), dma((Z,)), dma(()), dma(()),
         dma((H, 2)), dma((H, 2)), dma((H, 2)), dma((H, 2)),
         *spread_sems, *spread_sems,
         dma((Y,)), dma((Y,)), dma((XS,)), dma((XS,)), dma(()),
@@ -576,16 +604,16 @@
             jax.ShapeDtypeStruct((tokens, width), BF16),
             jax.ShapeDtypeStruct((15, 32, 128), F32),
         ),
-        in_specs=[hbm, hbm, hbm, hbm, hbm, smem, smem, vmem, vmem, vmem],
+        in_specs=[hbm] * 10,
         out_specs=(vmem, hbm),
         scratch_shapes=scratch,
         compiler_params=pltpu.CompilerParams(
-            collective_id=0, has_side_effects=True, vmem_limit_bytes=48 * 1024 * 1024),
+            collective_id=0, has_side_effects=True, vmem_limit_bytes=60 * 1024 * 1024),
         cost_estimate=pl.CostEstimate(
             flops=4 * tokens * depth * width, bytes_accessed=8 * tokens * depth, transcendentals=0),
     )(
-        activations.T, cotangent, next_inputs.T, weight_tiles.reshape(15, 32, 128),
-        momentum.reshape(15, 32, 128), chosen.reshape(8), counts.reshape(1),
+        activations.T, cotangent, next_inputs.T, weight_tiles,
+        momentum.reshape(15, 32, 128), chosen.reshape(1, 8), counts,
         jnp.asarray(fine), jnp.asarray(rows_low), jnp.asarray(cols_low),
     )
     return values, new_momentum.reshape(1, 15, TILE * TILE)

time: 91.9 us -> 84.1 us (0.915)
  local copies, waits for them, and re-layouts: 10.3 us -> 3.32 us
    unnamed x19 -> x2, local copies, waits for them, and re-layouts: 10.3 us -> 3.32 us
where the time goes in v2:
time: 84.1 us; the launch traced here: 83.9 us
  Pallas kernels  79.3 us (94%)
  local copies, waits for them, and re-layouts  3.32 us (4%)
  between operations  1.29 us (2%)
    pallas_call x1, Pallas kernels, local(): pl.pallas_call(functools.partial(kernel, Y, Z, scale), out_shape=(jax.Sha...  79.3 us
    unnamed x2, local copies, waits for them, and re-layouts  3.32 us

profile of v2, /device:TPU:1, one launch (start us, length us, event | category | flops | bytes accessed | tf_op | source)
XLA Modules:
  0.0 83.9 jit_solution(5749074734363431188)
XLA Ops:
  1.3 79.3 %shard_map.113 = (bf16[256,512]{1,0:T(8,128)(2,1)}, f32[15,32,128]{2,1,0:T(8,128)}) custom-call(bf16[2880,256]{1,0:T(8,128)(2,1)} %bitcast.6, bf16[256,512]{1,0:T(8,128)(2,1)} %cot_ref.1, bf16[2880,256]{1,0:T(8,128)(2,1)} %bitcast.7, bf16[15,4096]{1,0:T(8,128)(2,1)} %w_ref.1, f32[15,32,128]{2,1,0:T(8,128)} %bitcast.8, s32[1,8]{1,0:T(1,128)} %bitcast.9, ...), custom_call_target="tpu_custom_call" | custom-call | flops 1509949440 | bytes 5898240 | tf_op jit(solution)/shard_map/pallas_call | solution.py:601
  80.6 1.7 %copy.17 = bf16[256,512]{1,0:T(8,128)(2,1)} copy(bf16[256,512]{1,0:T(8,128)(2,1)} %get-tuple-element.12) | data formatting | bytes 524288
  82.3 1.7 %copy.18 = f32[1,15,4096]{2,0,1:T(1,128)} copy(f32[1,15,4096]{2,0,1:T(1,128)} %bitcast.5) | data formatting | bytes 491520

commit v3 on v2

--- a/solution.py
+++ b/solution.py
@@ -52,6 +52,10 @@
     rows_low = np.kron(np.eye(4, dtype=np.float32), low.T)
     cols_low = np.kron(np.eye(col_tiles, dtype=np.float32), low)
     return fine.astype(jnp.bfloat16), rows_low.astype(jnp.bfloat16), cols_low.astype(jnp.bfloat16)
+
+
+def far_first(size):
+    return sorted(range(1, size), key=lambda o: -min(o, size - o))
 
 
 def fold_sources(z_size, doubles):
@@ -94,24 +98,24 @@
 ):
     H = Z // 2
     ZS = Z // XS
-    UP = PAIRS // Y
+    UP = 2
     D = at_ref.shape[0]
     RT = D // TILE
     KB = xr.shape[1] // 256
     replica, tok = lax.axis_index("replica"), lax.axis_index("tok")
     y, x = replica // XS, replica % XS
     z, c = tok // 2, tok % 2
-    me = (replica, tok)
+    group = lax.rem(y, 4)
     sib = (replica, z * 2 + (1 - c))
 
     def at_z(o):
-        return (replica, ((z + o) % Z) * 2 + c)
+        return (replica, lax.rem(z + o, Z) * 2 + c)
 
     def at_y(o):
-        return (((y + o) % Y) * XS + x, tok)
+        return (lax.rem(y + o, Y) * XS + x, tok)
 
     def at_x(o):
-        return (y * XS + (x + o) % XS, tok)
+        return (y * XS + lax.rem(x + o, XS), tok)
 
     def rc(src, dst, ss, rs, dev):
         return pltpu.make_async_remote_copy(
@@ -184,7 +188,7 @@
             self.xs, self.xr, self.cs, self.cr = xs_, xr_, cs, cr
 
         def mine(self):
-            return self.buf.at[c, x, pl.ds(UP * y, UP)]
+            return self.buf.at[c, x, pl.ds(UP * group, UP)]
 
         def z_copy(self, o):
             part = self.mine().at[:, z // XS]
@@ -193,8 +197,7 @@
         def start_z(self):
             @pl.when(z % XS == x)
             def _():
-                @pl.loop(1, Z)
-                def _(o):
+                for o in far_first(Z):
                     self.z_copy(o).start()
 
         def wait_z(self):
@@ -205,19 +208,18 @@
                     part = self.mine().at[:, k]
                     rc(part, part, self.zs.at[0], self.zr.at[k], at_z(1)).wait_recv()
 
-        def y_copy(self, o):
-            return rc(self.mine(), self.mine(), self.ys.at[o - 1], self.yr.at[o - 1], at_y(o))
+        def y_copy(self, k):
+            return rc(self.mine(), self.mine(), self.ys.at[k], self.yr.at[k], at_y((2, 1, Y - 1)[k]))
 
         def start_y(self):
-            @pl.loop(1, Y)
-            def _(o):
-                self.y_copy(o).start()
+            for k in range(3):
+                self.y_copy(k).start()
 
         def wait_y(self):
-            @pl.loop(1, Y)
-            def _(o):
-                part = self.buf.at[c, x, pl.ds(UP * ((y + Y - o) % Y), UP)]
-                rc(part, part, self.ys.at[o - 1], self.yr.at[o - 1], at_y(1)).wait_recv()
+            for k in range(3):
+                source = lax.rem(group + (2, 3, 1)[k], 4)
+                part = self.buf.at[c, x, pl.ds(UP * source, UP)]
+                rc(part, part, self.ys.at[k], self.yr.at[k], at_y(1)).wait_recv()
 
         def x_copy(self, k):
             if k < 2:
@@ -265,9 +267,8 @@
                 def _(o):
                     self.z_copy(o).wait_send()
 
-            @pl.loop(1, Y)
-            def _(o):
-                self.y_copy(o).wait_send()
+            for k in range(3):
+                self.y_copy(k).wait_send()
 
             for k in range(4):
                 self.x_copy(k).wait_send()
@@ -281,25 +282,6 @@
         even = jnp.where(left, first, pltpu.roll(second, 64, 1))
         odd = jnp.where(left, pltpu.roll(first, 64, 1), second)
         return even, odd
-
-    loads[2].wait()
-
-    @pl.when(z % XS == x)
-    def _():
-        for k in range(UP):
-            number = 2 * (UP * y + k) - c
-            rows = lax.broadcasted_iota(jnp.int32, (15, 4096), 0)
-            for tile in range(2):
-                only = jnp.where(rows == number + tile, wfull[...].astype(F32), 0.0)
-                only = jnp.sum(only, axis=0, keepdims=True)
-                for r in range(32):
-                    wfold[tile, r:r + 1, :] = only[:, 128 * r:128 * r + 128]
-            even, odd = unfold(wfold[0], wfold[1])
-            wpair[pl.ds(0, 32, stride=2), :] = even
-            wpair[pl.ds(1, 32, stride=2), :] = odd
-            wall[c, x, UP * y + k, z // XS] = wpair[...].astype(BF16)
-
-    wide.start_z()
 
     loads[0].wait()
     loads[1].wait()
@@ -319,48 +301,71 @@
             row = pl.multiple_of((pair // 4) * TILE - start, TILE)
             own[slot, p] = prod[pair % 4, pl.ds(row, TILE), :]
 
-    def p_copy(s, h):
-        return rc(send_p.at[s, pl.ds(4 * h, 4)], got_p.at[s, pl.ds(4 * h, 4)],
-                  rp_send.at[s, h], rp_recv.at[s, h], at_z(1))
-
-    def m_copy(s, h):
-        return rc(send_m.at[s, pl.ds(4 * h, 4)], got_m.at[s, pl.ds(4 * h, 4)],
-                  rm_send.at[s, h], rm_recv.at[s, h], at_z(Z - 1))
+    def p_copy(s, q):
+        return rc(send_p.at[s, pl.ds(2 * q, 2)], got_p.at[s, pl.ds(2 * q, 2)],
+                  rp_send.at[s, q], rp_recv.at[s, q], at_z(1))
+
+    def m_copy(s, q):
+        return rc(send_m.at[s, pl.ds(2 * q, 2)], got_m.at[s, pl.ds(2 * q, 2)],
+                  rm_send.at[s, q], rm_recv.at[s, q], at_z(Z - 1))
 
     partial(H, 0)
-    send_p[0, 0:4] = own[0, 0:4].astype(BF16)
-    p_copy(0, 0).start()
-    send_m[0, 4:8] = own[0, 4:8].astype(BF16)
-    m_copy(0, 1).start()
-    wide.wait_z()
-    wide.start_y()
+    for k in range(2):
+        send_p[0, 2 * k:2 * k + 2] = own[0, 2 * k:2 * k + 2].astype(BF16)
+        p_copy(0, k).start()
+        send_m[0, 2 * k + 4:2 * k + 6] = own[0, 2 * k + 4:2 * k + 6].astype(BF16)
+        m_copy(0, k + 2).start()
     partial(H - 1, 2)
     partial(H + 1, 3)
+
+    loads[2].wait()
+
+    @pl.when(z % XS == x)
+    def _():
+        for k in range(UP):
+            number = 2 * (UP * group + k) - c
+            rows = lax.broadcasted_iota(jnp.int32, (15, 4096), 0)
+            for tile in range(2):
+                only = jnp.where(rows == number + tile, wfull[...].astype(F32), 0.0)
+                only = jnp.sum(only, axis=0, keepdims=True)
+                for r in range(32):
+                    wfold[tile, r:r + 1, :] = only[:, 128 * r:128 * r + 128]
+            even, odd = unfold(wfold[0], wfold[1])
+            wpair[pl.ds(0, 32, stride=2), :] = even
+            wpair[pl.ds(1, 32, stride=2), :] = odd
+            wall[c, x, UP * group + k, z // XS] = wpair[...].astype(BF16)
+
+    wide.start_z()
 
     @pl.loop(1, H)
     def _(s):
         now, later = 2 * (s % 2), 2 * ((s + 1) % 2)
 
-        def pass_on(copy, got, send, slot, h, first):
+        def pass_on(copy, got, send, slot, q, first):
             @pl.when(jnp.logical_or(s > 1, first))
             def _():
-                copy(s - 1, h).wait_recv()
-
-            part = own[slot, 4 * h:4 * h + 4] + got[s - 1, 4 * h:4 * h + 4].astype(F32)
-            send[s, 4 * h:4 * h + 4] = part.astype(BF16)
-            copy(s, h).start()
-
-        pass_on(p_copy, got_p, send_p, now, 0, True)
-        pass_on(m_copy, got_m, send_m, now + 1, 1, True)
-        partial(H - 1 - s, later)
-        pass_on(p_copy, got_p, send_p, now, 1, False)
-        pass_on(m_copy, got_m, send_m, now + 1, 0, False)
+                copy(s - 1, q).wait_recv()
+
+            part = own[slot, 2 * q:2 * q + 2] + got[s - 1, 2 * q:2 * q + 2].astype(F32)
+            send[s, 2 * q:2 * q + 2] = part.astype(BF16)
+            copy(s, q).start()
+
+        for k in range(4):
+            pass_on(p_copy, got_p, send_p, now, k, k < 2)
+            pass_on(m_copy, got_m, send_m, now + 1, (k + 2) % 4, k < 2)
+            if k == 1:
+                partial(H - 1 - s, later)
 
         @pl.when(s < H - 1)
         def _():
             partial(H + 1 + s, later + 1)
 
-        @pl.when(s == min(4, H - 1))
+        @pl.when(s == min(2, H - 1))
+        def _():
+            wide.wait_z()
+            wide.start_y()
+
+        @pl.when(s == min(5, H - 1))
         def _():
             wide.wait_y()
             wide.start_x()
@@ -389,9 +394,9 @@
         listed = jnp.where(s < counts_ref[0, 0], chosen_ref[0, s], -5)
         keep = jnp.where(number == listed, 1.0, keep)
 
-    for h in range(2):
-        p_copy(H - 1, h).wait_recv()
-        m_copy(H - 1, h).wait_recv()
+    for q in range(4):
+        p_copy(H - 1, q).wait_recv()
+        m_copy(H - 1, q).wait_recv()
     arrived = jnp.concatenate(
         [jnp.concatenate([got[H - 1, p] for p in range(PAIRS)], axis=1) for got in (got_p, got_m)], axis=0)
     side = dot(fine_ref[0:64, :], arrived)
@@ -410,20 +415,17 @@
         pack[2 * d + 1] = block[16:32]
 
     def ry_copy(o):
-        return rc(pack.at[pl.ds(UP * ((y + o) % Y), UP)], ys.at[o - 1],
+        return rc(pack.at[pl.ds(UP * lax.rem(lax.rem(y + o, Y), 4), UP)], ys.at[o - 1],
                   ry_send.at[o - 1], ry_recv.at[o - 1], at_y(o))
 
-    @pl.loop(1, Y)
-    def _(o):
+    for o in far_first(Y):
         ry_copy(o).start()
-
-    wide.forward_x()
 
     @pl.loop(1, Y)
     def _(o):
         ry_copy(o).wait_recv()
 
-    total = pack[pl.ds(UP * y, UP)].astype(F32)
+    total = pack[pl.ds(UP * group, UP)].astype(F32)
     for o in range(1, Y):
         total = total + ys[o - 1].astype(F32)
     xs[0] = total
@@ -431,7 +433,7 @@
     def rx_copy(o):
         return rc(xs.at[0], xs.at[o], rx_send.at[o - 1], rx_recv.at[o - 1], at_x(o))
 
-    for o in range(1, XS):
+    for o in far_first(XS):
         rx_copy(o).start()
 
     exact = quad.astype(BF16)
@@ -450,7 +452,7 @@
     @pl.when(z % XS == x)
     def _():
         for k in range(UP):
-            sall[c, x, UP * y + k, z // XS] = total[k].astype(BF16)
+            sall[c, x, UP * group + k, z // XS] = total[k].astype(BF16)
 
     quads.start_z()
 
@@ -462,12 +464,12 @@
     out_copy = pltpu.make_async_copy(nfold.at[pl.ds(1, 15)], newm_ref, out_sem)
     out_copy.start()
 
+    wide.forward_x()
     quads.wait_z()
     quads.start_y()
     loads[4].wait()
     loads[6].wait()
     loads[7].wait()
-    wide.finish_x()
 
     @pl.loop(0, KB)
     def _(k):
@@ -482,6 +484,7 @@
         rows = pl.ds(pl.multiple_of(256 * k, 256), 256)
         low_in[:, pl.ds(pl.multiple_of(128 * k, 128), 128)] = dot(xr[:, rows], rl_ref[...]).astype(BF16)
 
+    wide.finish_x()
     wide.wait_core()
     left64 = lax.broadcasted_iota(jnp.int32, (TILE, 128), 1) < 64
     for zz in range(Z):
@@ -528,14 +531,15 @@
     def _(e):
         a_copy(e).wait_send()
 
-    p_copy(0, 0).wait_send()
-    m_copy(0, 1).wait_send()
+    for k in range(2):
+        p_copy(0, k).wait_send()
+        m_copy(0, k + 2).wait_send()
 
     @pl.loop(1, H)
     def _(s):
-        for h in range(2):
-            p_copy(s, h).wait_send()
-            m_copy(s, h).wait_send()
+        for q in range(4):
+            p_copy(s, q).wait_send()
+            m_copy(s, q).wait_send()
 
     @pl.loop(1, Y)
     def _(o):
@@ -547,11 +551,24 @@
     quads.wait_sends()
 
 
+def hand_over(values_ref, newm_ref, values_out, newm_out, values_here, newm_here, sems):
+    moves = ((values_ref, values_here, values_out), (newm_ref, newm_here, newm_out))
+    fetched = [pltpu.make_async_copy(a, b, sems.at[k]) for k, (a, b, _) in enumerate(moves)]
+    stored = [pltpu.make_async_copy(b, d, sems.at[2 + k]) for k, (_, b, d) in enumerate(moves)]
+    for copy in fetched:
+        copy.start()
+    for before, copy in zip(fetched, stored):
+        before.wait()
+        copy.start()
+    for copy in stored:
+        copy.wait()
+
+
 def local(Y, Z, activations, cotangent, next_inputs, weight_tiles, momentum, chosen, counts):
     tokens, depth = activations.shape
     width = cotangent.shape[1]
     scale = 1.0 / math.sqrt(tokens * 2 * Z)
-    H, ZS, UP = Z // 2, Z // XS, PAIRS // Y
+    H, ZS, UP = Z // 2, Z // XS, 2
     KB = -(-depth // 256)
     fine, rows_low, cols_low = tables(width // TILE)
     hbm = pl.BlockSpec(memory_space=pl.ANY)
@@ -594,7 +611,7 @@
         pltpu.SMEM((1, 8), jnp.int32),
         pltpu.SMEM((1, 1), jnp.int32),
         dma((10,)), dma((Z,)), dma((Z,)), dma(()), dma(()),
-        dma((H, 2)), dma((H, 2)), dma((H, 2)), dma((H, 2)),
+        dma((H, 4)), dma((H, 4)), dma((H, 4)), dma((H, 4)),
         *spread_sems, *spread_sems,
         dma((Y,)), dma((Y,)), dma((XS,)), dma((XS,)), dma(()),
     ]
@@ -616,6 +633,17 @@
         momentum.reshape(15, 32, 128), chosen.reshape(1, 8), counts,
         jnp.asarray(fine), jnp.asarray(rows_low), jnp.asarray(cols_low),
     )
+    values, new_momentum = pl.pallas_call(
+        hand_over,
+        out_shape=(
+            jax.ShapeDtypeStruct(values.shape, values.dtype),
+            jax.ShapeDtypeStruct(new_momentum.shape, new_momentum.dtype),
+        ),
+        in_specs=[hbm, hbm],
+        out_specs=(hbm, hbm),
+        scratch_shapes=[pltpu.VMEM(values.shape, BF16), pltpu.VMEM(new_momentum.shape, F32), dma((4,))],
+        compiler_params=pltpu.CompilerParams(vmem_limit_bytes=60 * 1024 * 1024),
+    )(values, new_momentum)
     return values, new_momentum.reshape(1, 15, TILE * TILE)
 
 

time: 84.1 us -> 80.3 us (0.955)
  local copies, waits for them, and re-layouts: 3.32 us -> 0 us
    unnamed x2 -> x0, local copies, waits for them, and re-layouts: 3.32 us -> none
    pallas_call x1, Pallas kernels: 79.3 us -> 77.1 us  [local(): pl.pallas_call(functools.partial(kernel, Y, Z, scale), out_shape=(jax.Sha...]
    pallas_call x0 -> x1, Pallas kernels: none -> 1.76 us  [local(): pl.pallas_call(hand_over, out_shape=(jax.ShapeDtypeStruct(values.shape, v...]
where the time goes in v3:
time: 80.3 us; the launch traced here: 80.2 us
  Pallas kernels  78.9 us (98%)
  between operations  1.29 us (2%)
    pallas_call x1, Pallas kernels, local(): pl.pallas_call(functools.partial(kernel, Y, Z, scale), out_shape=(jax.Sha...  77.1 us
    pallas_call x1, Pallas kernels, local(): pl.pallas_call(hand_over, out_shape=(jax.ShapeDtypeStruct(values.shape, v...  1.76 us

profile of v3, /device:TPU:1, one launch (start us, length us, event | category | flops | bytes accessed | tf_op | source)
XLA Modules:
  0.0 80.2 jit_solution(12132970769030443636)
XLA Ops:
  1.3 77.1 %shard_map.113 = (bf16[256,512]{1,0:T(8,128)(2,1)}, f32[15,32,128]{2,1,0:T(8,128)}) custom-call(bf16[2880,256]{1,0:T(8,128)(2,1)} %bitcast.5, bf16[256,512]{1,0:T(8,128)(2,1)} %cot_ref.1, bf16[2880,256]{1,0:T(8,128)(2,1)} %bitcast.6, bf16[15,4096]{1,0:T(8,128)(2,1)} %w_ref.1, f32[15,32,128]{2,1,0:T(8,128)} %bitcast.7, s32[1,8]{1,0:T(1,128)} %bitcast.9, ...), custom_call_target="tpu_custom_call" | custom-call | flops 1509949440 | bytes 5898240 | tf_op jit(solution)/shard_map/pallas_call | solution.py:618
  78.4 1.8 %shard_map.114 = (bf16[256,512]{1,0:T(8,128)(2,1)}, f32[15,32,128]{2,1,0:T(8,128)}) custom-call(bf16[256,512]{1,0:T(8,128)(2,1)} %get-tuple-element.6.values_ref, f32[15,32,128]{2,1,0:T(8,128)} %get-tuple-element.7.newm_ref), custom_call_target="tpu_custom_call" | custom-call | tf_op jit(solution)/shard_map/pallas_call | solution.py:636

commit v4 on v3

--- a/solution.py
+++ b/solution.py
@@ -97,7 +97,6 @@
     ry_send, ry_recv, rx_send, rx_recv, out_sem,
 ):
     H = Z // 2
-    ZS = Z // XS
     UP = 2
     D = at_ref.shape[0]
     RT = D // TILE
@@ -161,49 +160,31 @@
         wmat[D:, :] = jnp.zeros((KB * 256 - D, wmat.shape[1]), BF16)
         smat[D // 2:, :] = jnp.zeros((KB * 128 - D // 2, smat.shape[1]), BF16)
 
-    pl.semaphore_wait(barrier, Z + Y + XS - 2)
-
-    def row_start(e, core):
-        dest = (z + e) % Z
-        return jnp.minimum((CHIP_PAIRS * dest + 7 * core) // 4, RT - 3) * TILE
-
-    def a_copy(e):
-        rows = pl.ds(pl.multiple_of(row_start(e, 1 - c), TILE), 3 * TILE)
-        return rc(at_ref.at[rows], a_sib.at[e], a_send.at[e], a_recv.at[e], sib)
-
-    c_copy = rc(cot_ref, c_sib, c_send, c_recv, sib)
-    c_copy.start()
-    a_copy(H).start()
-
-    @pl.loop(1, H)
-    def _(s):
-        a_copy(H - s).start()
-        a_copy(H + s).start()
-
-    a_copy(0).start()
-
     class Spread:
         def __init__(self, buf, zs_, zr, ys_, yr, xs_, xr_, cs, cr):
             self.buf, self.zs, self.zr, self.ys, self.yr = buf, zs_, zr, ys_, yr
             self.xs, self.xr, self.cs, self.cr = xs_, xr_, cs, cr
+            self.classes = buf.shape[1]
+            self.side = lax.rem(x, self.classes)
+            self.at_class = lax.rem(z, self.classes) == self.side
 
         def mine(self):
-            return self.buf.at[c, x, pl.ds(UP * group, UP)]
+            return self.buf.at[c, self.side, pl.ds(UP * group, UP)]
 
         def z_copy(self, o):
-            part = self.mine().at[:, z // XS]
-            return rc(part, part, self.zs.at[o - 1], self.zr.at[z // XS], at_z(o))
+            part = self.mine().at[:, z // self.classes]
+            return rc(part, part, self.zs.at[o - 1], self.zr.at[z // self.classes], at_z(o))
 
         def start_z(self):
-            @pl.when(z % XS == x)
+            @pl.when(self.at_class)
             def _():
                 for o in far_first(Z):
                     self.z_copy(o).start()
 
         def wait_z(self):
-            @pl.loop(0, ZS)
+            @pl.loop(0, Z // self.classes)
             def _(k):
-                @pl.when(z != x + XS * k)
+                @pl.when(z != self.side + self.classes * k)
                 def _():
                     part = self.mine().at[:, k]
                     rc(part, part, self.zs.at[0], self.zr.at[k], at_z(1)).wait_recv()
@@ -218,19 +199,28 @@
         def wait_y(self):
             for k in range(3):
                 source = lax.rem(group + (2, 3, 1)[k], 4)
-                part = self.buf.at[c, x, pl.ds(UP * source, UP)]
+                part = self.buf.at[c, self.side, pl.ds(UP * source, UP)]
                 rc(part, part, self.ys.at[k], self.yr.at[k], at_y(1)).wait_recv()
 
+        def half(self, core, side, k):
+            return self.buf.at[core, side, pl.ds(4 * k, 4)]
+
         def x_copy(self, k):
-            if k < 2:
-                part = self.buf.at[c, x]
+            if self.classes == 2:
+                part = self.half(c, self.side, k)
+            elif k < 2:
+                part = self.buf.at[c, self.side]
             else:
-                near = (x + XS - 1) % XS if k == 2 else (x + 1) % XS
-                part = self.buf.at[c, near, pl.ds(0 if k == 2 else 4, 4)]
-            return rc(part, part, self.xs.at[k], self.xr.at[k], at_x(1 if k % 2 == 0 else XS - 1))
+                part = self.half(c, lax.rem(x + (XS - 1, 1)[k - 2], XS), k - 2)
+            return rc(part, part, self.xs.at[k], self.xr.at[k], at_x((1, XS - 1)[k % 2]))
+
+        def core_parts(self, core):
+            if self.classes == 2:
+                return [self.buf.at[core, self.side], self.half(core, 1 - self.side, 0), self.half(core, 1 - self.side, 1)]
+            return [self.buf.at[core, lax.rem(x + o, XS)] for o in (0, XS - 1, 1, 2)]
 
         def c_copy(self, k):
-            part = self.buf.at[c, (x + k) % XS]
+            part = self.core_parts(c)[k]
             return rc(part, part, self.cs.at[k], self.cr.at[k], sib)
 
         def start_x(self):
@@ -238,30 +228,31 @@
             self.x_copy(1).start()
             self.c_copy(0).start()
 
+        def wait_x(self, part, k):
+            rc(part, part, self.xs.at[k], self.xr.at[k], at_x(1)).wait_recv()
+
         def forward_x(self):
-            from_left = self.buf.at[c, (x + XS - 1) % XS]
-            rc(from_left, from_left, self.xs.at[0], self.xr.at[0], at_x(1)).wait_recv()
-            self.x_copy(2).start()
-            self.c_copy(3).start()
-            from_right = self.buf.at[c, (x + 1) % XS]
-            rc(from_right, from_right, self.xs.at[1], self.xr.at[1], at_x(1)).wait_recv()
-            self.x_copy(3).start()
-            self.c_copy(1).start()
+            for k in range(2):
+                self.wait_x(self.buf.at[c, lax.rem(x + (XS - 1, 1)[k], XS)], k)
+                self.x_copy(2 + k).start()
+                self.c_copy(1 + k).start()
 
         def finish_x(self):
-            far = (x + 2) % XS
-            for k in (2, 3):
-                part = self.buf.at[c, far, pl.ds(0 if k == 2 else 4, 4)]
-                rc(part, part, self.xs.at[k], self.xr.at[k], at_x(1)).wait_recv()
-            self.c_copy(2).start()
+            for k in range(2):
+                if self.classes == 2:
+                    self.wait_x(self.half(c, 1 - self.side, k), k)
+                    self.c_copy(1 + k).start()
+                else:
+                    self.wait_x(self.half(c, lax.rem(x + 2, XS), k), 2 + k)
+            if self.classes == XS:
+                self.c_copy(3).start()
 
         def wait_core(self):
-            for k in range(XS):
-                part = self.buf.at[1 - c, (x + k) % XS]
+            for k, part in enumerate(self.core_parts(1 - c)):
                 rc(part, part, self.cs.at[k], self.cr.at[k], sib).wait_recv()
 
         def wait_sends(self):
-            @pl.when(z % XS == x)
+            @pl.when(self.at_class)
             def _():
                 @pl.loop(1, Z)
                 def _(o):
@@ -270,9 +261,9 @@
             for k in range(3):
                 self.y_copy(k).wait_send()
 
-            for k in range(4):
+            for k in range(2 if self.classes == 2 else 4):
                 self.x_copy(k).wait_send()
-            for k in range(XS):
+            for k in range(len(self.core_parts(c))):
                 self.c_copy(k).wait_send()
 
     wide = Spread(wall, wz_send, wz_recv, wy_send, wy_recv, wx_send, wx_recv, wc_send, wc_recv)
@@ -282,6 +273,40 @@
         even = jnp.where(left, first, pltpu.roll(second, 64, 1))
         odd = jnp.where(left, pltpu.roll(first, 64, 1), second)
         return even, odd
+
+    loads[2].wait()
+
+    @pl.when(wide.at_class)
+    def _():
+        for k in range(UP):
+            number = 2 * (UP * group + k) - c
+            rows = lax.broadcasted_iota(jnp.int32, (15, 4096), 0)
+            for tile in range(2):
+                only = jnp.where(rows == number + tile, wfull[...].astype(F32), 0.0)
+                only = jnp.sum(only, axis=0, keepdims=True)
+                for r in range(32):
+                    wfold[tile, r:r + 1, :] = only[:, 128 * r:128 * r + 128]
+            even, odd = unfold(wfold[0], wfold[1])
+            wpair[pl.ds(0, 32, stride=2), :] = even
+            wpair[pl.ds(1, 32, stride=2), :] = odd
+            wall[c, wide.side, UP * group + k, z // XS] = wpair[...].astype(BF16)
+
+    pl.semaphore_wait(barrier, Z + Y + XS - 2)
+
+    def row_start(e, core):
+        dest = (z + e) % Z
+        return jnp.minimum((CHIP_PAIRS * dest + 7 * core) // 4, RT - 3) * TILE
+
+    def a_copy(e):
+        rows = pl.ds(pl.multiple_of(row_start(e, 1 - c), TILE), 3 * TILE)
+        return rc(at_ref.at[rows], a_sib.at[e], a_send.at[e], a_recv.at[e], sib)
+
+    c_copy = rc(cot_ref, c_sib, c_send, c_recv, sib)
+    c_copy.start()
+    a_copy(H).start()
+
+    a_copy(H - 1).start()
+    a_copy(H + 1).start()
 
     loads[0].wait()
     loads[1].wait()
@@ -315,25 +340,15 @@
         p_copy(0, k).start()
         send_m[0, 2 * k + 4:2 * k + 6] = own[0, 2 * k + 4:2 * k + 6].astype(BF16)
         m_copy(0, k + 2).start()
+
+    @pl.loop(2, H)
+    def _(s):
+        a_copy(H - s).start()
+        a_copy(H + s).start()
+
+    a_copy(0).start()
     partial(H - 1, 2)
     partial(H + 1, 3)
-
-    loads[2].wait()
-
-    @pl.when(z % XS == x)
-    def _():
-        for k in range(UP):
-            number = 2 * (UP * group + k) - c
-            rows = lax.broadcasted_iota(jnp.int32, (15, 4096), 0)
-            for tile in range(2):
-                only = jnp.where(rows == number + tile, wfull[...].astype(F32), 0.0)
-                only = jnp.sum(only, axis=0, keepdims=True)
-                for r in range(32):
-                    wfold[tile, r:r + 1, :] = only[:, 128 * r:128 * r + 128]
-            even, odd = unfold(wfold[0], wfold[1])
-            wpair[pl.ds(0, 32, stride=2), :] = even
-            wpair[pl.ds(1, 32, stride=2), :] = odd
-            wall[c, x, UP * group + k, z // XS] = wpair[...].astype(BF16)
 
     wide.start_z()
 
@@ -364,11 +379,6 @@
         def _():
             wide.wait_z()
             wide.start_y()
-
-        @pl.when(s == min(5, H - 1))
-        def _():
-            wide.wait_y()
-            wide.start_x()
 
     last = 2 * (H % 2)
 
@@ -394,6 +404,8 @@
         listed = jnp.where(s < counts_ref[0, 0], chosen_ref[0, s], -5)
         keep = jnp.where(number == listed, 1.0, keep)
 
+    wide.wait_y()
+    wide.start_x()
     for q in range(4):
         p_copy(H - 1, q).wait_recv()
         m_copy(H - 1, q).wait_recv()
@@ -449,10 +461,10 @@
         rx_copy(o).wait_recv()
     total = (xs[0] + xs[2]) + (xs[1] + xs[3])
 
-    @pl.when(z % XS == x)
+    @pl.when(quads.at_class)
     def _():
         for k in range(UP):
-            sall[c, x, UP * group + k, z // XS] = total[k].astype(BF16)
+            sall[c, quads.side, UP * group + k, z // 2] = total[k].astype(BF16)
 
     quads.start_z()
 
@@ -478,13 +490,13 @@
 
     quads.wait_y()
     quads.start_x()
+    wide.finish_x()
 
     @pl.loop(0, KB)
     def _(k):
         rows = pl.ds(pl.multiple_of(256 * k, 256), 256)
         low_in[:, pl.ds(pl.multiple_of(128 * k, 128), 128)] = dot(xr[:, rows], rl_ref[...]).astype(BF16)
 
-    wide.finish_x()
     wide.wait_core()
     left64 = lax.broadcasted_iota(jnp.int32, (TILE, 128), 1) < 64
     for zz in range(Z):
@@ -497,7 +509,6 @@
             wmat[TILE * (pair // 4):TILE * (pair // 4) + TILE,
                  128 * (pair % 4):128 * (pair % 4) + 128] = block
 
-    quads.forward_x()
     base[...] = jnp.zeros(base.shape, F32)
 
     @pl.loop(0, KB)
@@ -513,7 +524,7 @@
         for half in range(2):
             block = None
             for (core, zz, d), (lo, hi) in parts:
-                part = sall[core, zz % XS, 2 * d + half, zz // XS]
+                part = sall[core, zz % 2, 2 * d + half, zz // 2]
                 if block is None:
                     block = part
                 else:
@@ -568,13 +579,13 @@
     tokens, depth = activations.shape
     width = cotangent.shape[1]
     scale = 1.0 / math.sqrt(tokens * 2 * Z)
-    H, ZS, UP = Z // 2, Z // XS, 2
+    H, UP = Z // 2, 2
     KB = -(-depth // 256)
     fine, rows_low, cols_low = tables(width // TILE)
     hbm = pl.BlockSpec(memory_space=pl.ANY)
     vmem = pl.BlockSpec(memory_space=pltpu.VMEM)
     dma = pltpu.SemaphoreType.DMA
-    spread_sems = [dma((Z - 1,)), dma((ZS,)), dma((Y,)), dma((Y,)), dma((4,)), dma((4,)), dma((4,)), dma((4,))]
+    spread_sems = [dma((Z - 1,)), dma((Z // 2,)), dma((Y,)), dma((Y,)), dma((4,)), dma((4,)), dma((4,)), dma((4,))]
     pairs = (PAIRS, TILE, 128)
     scratch = [
         pltpu.VMEM((depth, tokens), BF16),
@@ -584,7 +595,7 @@
         pltpu.VMEM((KB * 256, tokens), BF16),
         pltpu.VMEM((tokens, KB * 256), BF16),
         pltpu.VMEM((tokens, KB * 128), BF16),
-        pltpu.VMEM((2, XS, PAIRS, ZS, TILE, 128), BF16),
+        pltpu.VMEM((2, XS, PAIRS, Z // XS, TILE, 128), BF16),
         pltpu.VMEM((KB * 256, width), BF16),
         pltpu.VMEM((15, TILE * TILE), BF16),
         pltpu.VMEM((2, 32, 128), F32),
@@ -601,7 +612,7 @@
         pltpu.VMEM((8, 16, 128), BF16),
         pltpu.VMEM((Y, UP, 16, 128), BF16),
         pltpu.VMEM((XS, UP, 16, 128), F32),
-        pltpu.VMEM((2, XS, PAIRS, ZS, 16, 128), BF16),
+        pltpu.VMEM((2, 2, PAIRS, Z // 2, 16, 128), BF16),
         pltpu.VMEM((KB * 128, width // 2), BF16),
         pltpu.VMEM((tokens, width), F32),
         pltpu.VMEM((17, 32, 128), F32),

time: 80.3 us -> 80 us (level)
  no operation moved by 1% of the time
where the time goes in v4:
time: 80 us; the launch traced here: 79.9 us
  Pallas kernels  78.6 us (98%)
  between operations  1.29 us (2%)
    pallas_call x1, Pallas kernels, local(): pl.pallas_call(functools.partial(kernel, Y, Z, scale), out_shape=(jax.Sha...  76.8 us
    pallas_call x1, Pallas kernels, local(): pl.pallas_call(hand_over, out_shape=(jax.ShapeDtypeStruct(values.shape, v...  1.76 us

profile of v4, /device:TPU:1, one launch (start us, length us, event | category | flops | bytes accessed | tf_op | source)
XLA Modules:
  0.0 79.9 jit_solution(2849627288449693809)
XLA Ops:
  1.3 76.8 %shard_map.113 = (bf16[256,512]{1,0:T(8,128)(2,1)}, f32[15,32,128]{2,1,0:T(8,128)}) custom-call(bf16[2880,256]{1,0:T(8,128)(2,1)} %bitcast.5, bf16[256,512]{1,0:T(8,128)(2,1)} %cot_ref.1, bf16[2880,256]{1,0:T(8,128)(2,1)} %bitcast.6, bf16[15,4096]{1,0:T(8,128)(2,1)} %w_ref.1, f32[15,32,128]{2,1,0:T(8,128)} %bitcast.7, s32[1,8]{1,0:T(1,128)} %bitcast.9, ...), custom_call_target="tpu_custom_call" | custom-call | flops 1509949440 | bytes 5898240 | tf_op jit(solution)/shard_map/pallas_call | solution.py:629
  78.1 1.8 %shard_map.114 = (bf16[256,512]{1,0:T(8,128)(2,1)}, f32[15,32,128]{2,1,0:T(8,128)}) custom-call(bf16[256,512]{1,0:T(8,128)(2,1)} %get-tuple-element.6.values_ref, f32[15,32,128]{2,1,0:T(8,128)} %get-tuple-element.7.newm_ref), custom_call_target="tpu_custom_call" | custom-call | tf_op jit(solution)/shard_map/pallas_call | solution.py:647

commit v5 on v4

--- a/solution.py
+++ b/solution.py
@@ -261,6 +261,7 @@
             for k in range(3):
                 self.y_copy(k).wait_send()
 
+        def wait_late_sends(self):
             for k in range(2 if self.classes == 2 else 4):
                 self.x_copy(k).wait_send()
             for k in range(len(self.core_parts(c))):
@@ -433,6 +434,22 @@
     for o in far_first(Y):
         ry_copy(o).start()
 
+    c_copy.wait_send()
+
+    @pl.loop(0, Z)
+    def _(e):
+        a_copy(e).wait_send()
+
+    for k in range(2):
+        p_copy(0, k).wait_send()
+        m_copy(0, k + 2).wait_send()
+
+    @pl.loop(1, H)
+    def _(s):
+        for q in range(4):
+            p_copy(s, q).wait_send()
+            m_copy(s, q).wait_send()
+
     @pl.loop(1, Y)
     def _(o):
         ry_copy(o).wait_recv()
@@ -476,6 +493,13 @@
     out_copy = pltpu.make_async_copy(nfold.at[pl.ds(1, 15)], newm_ref, out_sem)
     out_copy.start()
 
+    @pl.loop(1, Y)
+    def _(o):
+        ry_copy(o).wait_send()
+
+    for o in range(1, XS):
+        rx_copy(o).wait_send()
+    wide.wait_sends()
     wide.forward_x()
     quads.wait_z()
     quads.start_y()
@@ -516,6 +540,8 @@
         rows = pl.ds(pl.multiple_of(256 * k, 256), 256)
         base[...] += dot(xr[:, rows], wmat[rows, :])
 
+    wide.wait_late_sends()
+    quads.wait_sends()
     quads.finish_x()
     quads.wait_core()
 
@@ -536,30 +562,7 @@
     values_ref[...] = (base[...] - dot(late.astype(BF16), cl_ref[...])).astype(BF16)
 
     out_copy.wait()
-    c_copy.wait_send()
-
-    @pl.loop(0, Z)
-    def _(e):
-        a_copy(e).wait_send()
-
-    for k in range(2):
-        p_copy(0, k).wait_send()
-        m_copy(0, k + 2).wait_send()
-
-    @pl.loop(1, H)
-    def _(s):
-        for q in range(4):
-            p_copy(s, q).wait_send()
-            m_copy(s, q).wait_send()
-
-    @pl.loop(1, Y)
-    def _(o):
-        ry_copy(o).wait_send()
-
-    for o in range(1, XS):
-        rx_copy(o).wait_send()
-    wide.wait_sends()
-    quads.wait_sends()
+    quads.wait_late_sends()
 
 
 def hand_over(values_ref, newm_ref, values_out, newm_out, values_here, newm_here, sems):

time: 80 us -> 79.8 us (level)
  no operation moved by 1% of the time
where the time goes in v5:
time: 79.8 us; the launch traced here: 79.6 us
  Pallas kernels  78.3 us (98%)
  between operations  1.29 us (2%)
    pallas_call x1, Pallas kernels, local(): pl.pallas_call(functools.partial(kernel, Y, Z, scale), out_shape=(jax.Sha...  76.6 us
    pallas_call x1, Pallas kernels, local(): pl.pallas_call(hand_over, out_shape=(jax.ShapeDtypeStruct(values.shape, v...  1.76 us

profile of v5, /device:TPU:1, one launch (start us, length us, event | category | flops | bytes accessed | tf_op | source)
XLA Modules:
  0.0 79.6 jit_solution(8497821675296464563)
XLA Ops:
  1.3 76.6 %shard_map.113 = (bf16[256,512]{1,0:T(8,128)(2,1)}, f32[15,32,128]{2,1,0:T(8,128)}) custom-call(bf16[2880,256]{1,0:T(8,128)(2,1)} %bitcast.5, bf16[256,512]{1,0:T(8,128)(2,1)} %cot_ref.1, bf16[2880,256]{1,0:T(8,128)(2,1)} %bitcast.6, bf16[15,4096]{1,0:T(8,128)(2,1)} %w_ref.1, f32[15,32,128]{2,1,0:T(8,128)} %bitcast.7, s32[1,8]{1,0:T(1,128)} %bitcast.9, ...), custom_call_target="tpu_custom_call" | custom-call | flops 1509949440 | bytes 5898240 | tf_op jit(solution)/shard_map/pallas_call | solution.py:632
  77.9 1.8 %shard_map.114 = (bf16[256,512]{1,0:T(8,128)(2,1)}, f32[15,32,128]{2,1,0:T(8,128)}) custom-call(bf16[256,512]{1,0:T(8,128)(2,1)} %get-tuple-element.6.values_ref, f32[15,32,128]{2,1,0:T(8,128)} %get-tuple-element.7.newm_ref), custom_call_target="tpu_custom_call" | custom-call | tf_op jit(solution)/shard_map/pallas_call | solution.py:650
